TPU v7x, 512 devices: a whole 4x8x8 slice. The times are simulated.
512 devices in a mesh: dp: 8 (over z_lo, core), ctx: 64 (over y, z_hi, x).
Axes of the slice: x: 4, y: 8, z: 8 (z_hi: 2, z_lo: 4; z = z_hi * 4 + z_lo), core: 2. Of those that a mesh axis runs over, the one named last changes fastest.
Arguments:
- token_ids: int32 [8, 16384], P('dp'), may hold values from 0 to 30527
- target_ids: int32 [8], replicated, may hold values from 0 to 127
- candidates: int32 [4], replicated, may hold values from 0 to 7
- embed_table: bfloat16 [1536, 30528], P('ctx'), may hold values from -6 to 6
- online_blocks: bfloat16 [64, 256, 256], P('ctx'), may hold values from -0.375 to 0.375
- online_across: bfloat16 [256, 64, 64], P('ctx'), may hold values from -0.75 to 0.75
- online_channel: bfloat16 [2, 4, 384, 384], P(None, None, 'dp'), may hold values from -0.3125 to 0.3125
- online_gain: bfloat16 [1536], replicated, may hold values from 0.099609375 to 1.8984375
- online_head: bfloat16 [1536, 128], P('dp'), may hold values from -2 to 2
- ref_blocks: bfloat16 [64, 256, 256], P('ctx'), may hold values from -0.375 to 0.375
- ref_across: bfloat16 [256, 64, 64], P('ctx'), may hold values from -0.75 to 0.75
- ref_channel: bfloat16 [2, 4, 384, 384], P(None, None, 'dp'), may hold values from -0.3125 to 0.3125
- ref_gain: bfloat16 [1536], replicated, may hold values from 0.099609375 to 1.8984375
- ref_head: bfloat16 [1536, 128], P('dp'), may hold values from -2 to 2
Outputs:
- online_out: bfloat16 [131072, 1536], P(('dp', 'ctx'))
- scores: float32 [8], replicated
- picked: float32 [4], replicated
All inputs are finite; a program needn't handle non-finite values.
Results may differ from a plain program's by a relative error of at most 0.005.
Values may be sent and summed in bfloat16 or wider, within the bound.
A program may use at most 64 MiB of HBM per device.

v0:
```python
import jax
import jax.numpy as jnp
from jax import lax
from jax.sharding import PartitionSpec as P


def channel_gate(normed_h, channel):
    tok_rows = normed_h.shape[0]
    block_count = channel.shape[1]
    block_width = channel.shape[2]
    section_one = jnp.einsum(
        "tki,kij->tkj",
        normed_h.reshape(tok_rows, block_count, block_width),
        channel[0],
        preferred_element_type=jnp.float32,
    ).astype(jnp.bfloat16)
    section_one = section_one.reshape(
        tok_rows, block_count, block_count, block_width // block_count
    )
    factor_two = channel[1].reshape(
        block_count, block_width // block_count, block_count, block_width
    )
    section_two = jnp.einsum(
        "tkqj,qjko->tqo", section_one, factor_two, preferred_element_type=jnp.float32
    )
    return jax.nn.sigmoid(section_two.reshape(tok_rows, block_count * block_width))


def normed(tokens, gain):
    xfloat = tokens.astype(jnp.float32)
    scaled = (
        xfloat
        * lax.rsqrt(jnp.mean(xfloat * xfloat, axis=-1, keepdims=True) + 1e-06)
        * gain.astype(jnp.float32)
    )
    return scaled.astype(jnp.bfloat16)


def within_blocks(normed_h, blocks):
    block_size = blocks.shape[1]
    shaped = normed_h.reshape(blocks.shape[0], block_size, normed_h.shape[1])
    return jnp.einsum("aoi,aic->aoc", blocks, shaped, preferred_element_type=jnp.float32).astype(
        jnp.bfloat16
    )


def run_models(tokens, member_set):
    channel_stack = jnp.stack([member[2] for member in member_set])
    head_stack = jnp.stack([member[4] for member in member_set])[:, None, None]
    channel_sets, head_sets = (
        lax.all_gather(channel_stack, "dp", axis=3, tiled=True),
        lax.all_gather(head_stack, "dp", axis=3, tiled=True),
    )
    normed_list = [normed(tokens, member[3]) for member in member_set]
    within = jnp.stack([within_blocks(normed_list[0], member_set[0][0])])
    columns = lax.all_to_all(within, "ctx", split_axis=2, concat_axis=1, tiled=True)
    mixed_cols = jnp.stack(
        [
            jnp.einsum(
                "bqa,abc->qbc", member_set[0][1], columns[0], preferred_element_type=jnp.float32
            ).astype(jnp.bfloat16)
        ]
    )
    returned = lax.all_to_all(mixed_cols, "ctx", split_axis=1, concat_axis=2, tiled=True)
    xfloat = tokens.astype(jnp.float32)
    gate = channel_gate(normed_list[0], channel_sets[0])
    mixed_rows = returned[0].reshape(tokens.shape).astype(jnp.float32)
    outputs = [(xfloat + mixed_rows * gate).astype(jnp.bfloat16)]
    return (outputs, head_sets[:, 0, 0])


def body(
    token_ids,
    target_ids,
    candidates,
    embed_table,
    online_blocks,
    online_across,
    online_channel,
    online_gain,
    online_head,
    ref_blocks,
    ref_across,
    ref_channel,
    ref_gain,
    ref_head,
):
    looked_up = jnp.take(embed_table, token_ids[0], axis=1)
    features = lax.all_to_all(looked_up, "ctx", split_axis=1, concat_axis=0, tiled=True)
    tokens = features.T
    online = (online_blocks, online_across, online_channel, online_gain, online_head)
    frozen = (ref_blocks, ref_across, ref_channel, ref_gain, ref_head)
    batches = ((online,), (frozen,))
    results = []
    head_list = []
    for member_set in batches:
        outputs, head_sets = run_models(tokens, member_set)
        results.extend(outputs)
        head_list.append(head_sets)
    head_all = jnp.concatenate(head_list, axis=0).astype(jnp.float32)
    local_sums = jnp.stack([jnp.sum(output.astype(jnp.float32), axis=0) for output in results])
    n_seqs = lax.axis_size("dp")
    own_row = lax.axis_index("dp")
    mine = (jnp.arange(n_seqs, dtype=jnp.int32) == own_row).astype(jnp.float32)
    contribution = mine[:, None, None] * local_sums[None]
    totals = lax.psum(contribution, ("dp", "ctx"))
    seq_len = token_ids.shape[1]
    pooled = totals / seq_len
    normalized = pooled * lax.rsqrt(jnp.mean(pooled * pooled, axis=-1, keepdims=True) + 1e-06)
    logits = jnp.einsum("nmd,mdc->nmc", normalized, head_all, precision=lax.Precision.HIGHEST)
    total_exp = jax.nn.logsumexp(logits, axis=-1)
    target_mask = (
        target_ids[:, None] == jnp.arange(logits.shape[2], dtype=jnp.int32)[None]
    ).astype(jnp.float32)
    chosen = jnp.sum(logits * target_mask[:, None, :], axis=-1)
    losses = total_exp - chosen
    scores = losses[:, 0] - losses[:, 1]
    pick_mask = (candidates[:, None] == jnp.arange(n_seqs, dtype=jnp.int32)[None]).astype(
        jnp.float32
    )
    picked = jnp.sum(pick_mask * scores[None], axis=1)
    return (results[0], scores, picked)


def solution(mesh):
    in_specs = (
        P("dp", None),
        P(),
        P(),
        P("ctx", None),
        P("ctx", None, None),
        P("ctx", None, None),
        P(None, None, "dp", None),
        P(),
        P("dp", None),
        P("ctx", None, None),
        P("ctx", None, None),
        P(None, None, "dp", None),
        P(),
        P("dp", None),
    )
    out_specs = (P(("dp", "ctx"), None), P(), P())
    return jax.shard_map(body, mesh=mesh, in_specs=in_specs, out_specs=out_specs, check_vma=False)
```

profile of v0, /device:TPU:1, one launch (start us, length us, event | category | flops | bytes accessed | tf_op | source)
XLA Modules:
  0.0 578.1 jit_solution(15232764407401268444)
XLA Ops:
  7.9 6.7 %copy.67 = bf16[24,30528]{0,1:T(8,128)(2,1)} copy(bf16[24,30528]{1,0:T(8,128)(2,1)} %param.17) | data formatting | bytes 2930688 | tf_op args[3]
  14.8 59.6 %gather_fusion = bf16[16384,24]{1,0:T(8,128)(2,1)} fusion(bf16[24,30528]{0,1:T(8,128)(2,1)} %copy.67, s32[16384]{0:T(1024)S(1)} %broadcast_clamp_fusion), kind=kCustom, calls=%fused_computation | custom fusion | bytes 1638400 | tf_op jit(solution)/shard_map/jit(_take)/gather | solution.py:88
  74.4 3.5 copy.68
  80.2 19.6 %all-to-all-start = ((bf16[24,64,256]{2,0,1:T(8,128)(2,1)}), bf16[24,64,256]{2,0,1:T(8,128)(2,1)S(1)}, u32[]{:S(2)}, u32[]{:S(2)}) async-start(bf16[24,64,256]{2,0,1:T(8,128)(2,1)} %broadcast_select_fusion), calls=%async_computation | async-start | bytes 1572864 | tf_op jit(solution)/shard_map/all_to_all | solution.py:89
  99.8 23.2 %all-to-all-done = bf16[24,64,256]{2,0,1:T(8,128)(2,1)S(1)} async-done(((bf16[24,64,256]{2,0,1:T(8,128)(2,1)}), bf16[24,64,256]{2,0,1:T(8,128)(2,1)S(1)}, u32[]{:S(2)}, u32[]{:S(2)}) %all-to-all-start) | async-done | bytes 786464 | tf_op jit(solution)/shard_map/all_to_all | solution.py:89
  124.2 3.1 copy.69
  127.8 6.4 %reduce.8 = bf16[256,1536]{1,0:T(8,128)(2,1)S(1)} reduce(bf16[256,1,1,1536]{3,2,1,0:T(2,128)(2,1)} %bitcast.135, bf16[]{:T(256)} %broadcast.142), dimensions={1,2}, to_apply=%bitcast.117.reduce_sub_computation | reduce | bytes 1572866
  135.6 9.4 %all-to-all-start.1 = ((bf16[64,2,3072]{2,1,0:T(2,128)(2,1)}), bf16[64,2,3072]{2,1,0:T(2,128)(2,1)}, u32[]{:S(2)}, u32[]{:S(2)}) async-start(bf16[64,2,3072]{2,1,0:T(2,128)(2,1)} %reshape.216), calls=%async_computation.1 | async-start | bytes 1572864 | tf_op jit(solution)/shard_map/all_to_all | solution.py:56
  146.1 3.1 copy.77
  149.2 6.4 %reduce.9 = bf16[256,1536]{1,0:T(8,128)(2,1)S(1)} reduce(bf16[256,1,1,1536]{3,2,1,0:T(2,128)(2,1)} %bitcast.136, bf16[]{:T(256)} %broadcast.142), dimensions={1,2}, to_apply=%bitcast.119.reduce_sub_computation | reduce | bytes 1572866
  157.0 10.7 %all-to-all-done.1 = bf16[64,2,3072]{2,1,0:T(2,128)(2,1)} async-done(((bf16[64,2,3072]{2,1,0:T(2,128)(2,1)}), bf16[64,2,3072]{2,1,0:T(2,128)(2,1)}, u32[]{:S(2)}, u32[]{:S(2)}) %all-to-all-start.1) | async-done | bytes 786464 | tf_op jit(solution)/shard_map/all_to_all | solution.py:56
  167.8 9.9 %all-to-all-start.3 = ((bf16[64,2,3072]{2,1,0:T(2,128)(2,1)}), bf16[64,2,3072]{2,1,0:T(2,128)(2,1)}, u32[]{:S(2)}, u32[]{:S(2)}) async-start(bf16[64,2,3072]{2,1,0:T(2,128)(2,1)} %reshape.218), calls=%async_computation.3 | async-start | bytes 1572864 | tf_op jit(solution)/shard_map/all_to_all | solution.py:56
  177.7 5.8 %reshape.217 = bf16[256,1,1,1536]{3,2,1,0:T(2,128)(2,1)} reshape(bf16[64,2,3072]{2,1,0:T(2,128)(2,1)} %all-to-all-done.1) | data formatting | bytes 1572864
  183.5 6.9 %bitcast_reduce_fusion.1 = bf16[256,1536]{1,0:T(8,128)(2,1)} fusion(bf16[256,1,1,1536]{3,2,1,0:T(2,128)(2,1)} %reshape.217), kind=kLoop, calls=%fused_computation.75 | loop fusion | bytes 1572864 | tf_op jit(solution)/shard_map/all_to_all | solution.py:56
  194.0 5.7 all-to-all-done.3
  199.7 9.3 %all-to-all-start.2 = ((bf16[1,64,4,1536]{3,2,0,1:T(4,128)(2,1)}), bf16[1,64,4,1536]{3,2,0,1:T(4,128)(2,1)}, u32[]{:S(2)}, u32[]{:S(2)}) async-start(bf16[1,64,4,1536]{3,2,0,1:T(4,128)(2,1)} %copy.71), calls=%async_computation.2 | async-start | bytes 1572864 | tf_op jit(solution)/shard_map/all_to_all | solution.py:64
  209.2 5.8 %reshape.219 = bf16[256,1,1,1536]{3,2,1,0:T(2,128)(2,1)} reshape(bf16[64,2,3072]{2,1,0:T(2,128)(2,1)} %all-to-all-done.3) | data formatting | bytes 1572864
  215.0 6.9 %bitcast_reduce_fusion = bf16[256,1536]{1,0:T(8,128)(2,1)} fusion(bf16[256,1,1,1536]{3,2,1,0:T(2,128)(2,1)} %reshape.219), kind=kLoop, calls=%fused_computation.74 | loop fusion | bytes 1572864 | tf_op jit(solution)/shard_map/all_to_all | solution.py:56
  225.5 3.4 all-to-all-done.2
  229.0 11.5 %all-to-all-start.4 = ((bf16[1,64,4,1536]{3,2,0,1:T(4,128)(2,1)}), bf16[1,64,4,1536]{3,2,0,1:T(4,128)(2,1)}, u32[]{:S(2)}, u32[]{:S(2)}) async-start(bf16[1,64,4,1536]{3,2,0,1:T(4,128)(2,1)} %copy.79), calls=%async_computation.4 | async-start | bytes 1572864 | tf_op jit(solution)/shard_map/all_to_all | solution.py:64
  240.5 34.4 %all-gather.1 = bf16[1536,128]{1,0:T(8,128)(2,1)} all-gather(bf16[192,128]{1,0:T(8,128)(2,1)S(1)} %copy-done.10), channel_id=3, replica_groups=mesh['dp'=8,'ctx'=64] {'dp'}, dimensions={0}, use_global_device_ids=true | all-gather | bytes 442368 | tf_op jit(solution)/shard_map/all_gather | solution.py:52
  303.8 3.4 convert_reduce_fusion.1
  308.0 14.6 %all-gather.2 = bf16[1536,128]{1,0:T(8,128)(2,1)S(1)} all-gather(bf16[192,128]{1,0:T(8,128)(2,1)S(1)} %copy-done.11), channel_id=4, replica_groups=mesh['dp'=8,'ctx'=64] {'dp'}, dimensions={0}, use_global_device_ids=true | all-gather | bytes 442368 | tf_op jit(solution)/shard_map/all_gather | solution.py:52
  323.8 244.2 %all-reduce.2.cloned.1.call-done = f32[8,2,1536]{2,0,1:T(8,128)} async-done(((f32[8,2,1536]{2,0,1:T(8,128)}), f32[8,2,1536]{2,0,1:T(8,128)}) %all-reduce.2.cloned.1.call-update) | async-done | bytes 98320 | tf_op jit(solution)/shard_map/psum | solution.py:106
  (97 shorter events, 50.1 us)
Async XLA Ops:
  7.2 116.6 %copy-start = (bf16[1,256,256]{2,1,0:T(8,128)(2,1)S(1)}, bf16[1,256,256]{2,1,0:T(8,128)(2,1)}, u32[]{:S(2)}) copy-start(bf16[1,256,256]{2,1,0:T(8,128)(2,1)} %param.18) | copy-start | bytes 393220
  7.2 267.7 %all-gather.7.cloned.1.call-start = ((), (), s32[]{:S(2)}) async-start(), calls=%async_computation.6 | async-start | bytes 2654208 | tf_op jit(solution)/shard_map/all_gather | solution.py:51
  7.9 6.7 %copy-start.6 = (s32[1,16384]{1,0:T(1,128)S(1)}, s32[1,16384]{1,0:T(1,128)}, u32[]{:S(2)}) copy-start(s32[1,16384]{1,0:T(1,128)} %param.14) | copy-start | bytes 196612
  79.2 20.6 %copy-start.12 = (bf16[1536]{0:T(1024)(128)(2,1)S(1)}, bf16[1536]{0:T(1024)(128)(2,1)}, u32[]{:S(2)}) copy-start(bf16[1536]{0:T(1024)(128)(2,1)} %param.21) | copy-start | bytes 9220
  79.2 20.6 %copy-start.13 = (bf16[1536]{0:T(1024)(128)(2,1)S(1)}, bf16[1536]{0:T(1024)(128)(2,1)}, u32[]{:S(2)}) copy-start(bf16[1536]{0:T(1024)(128)(2,1)} %param.26) | copy-start | bytes 9220
  80.2 42.8 %all-to-all-start = ((bf16[24,64,256]{2,0,1:T(8,128)(2,1)}), bf16[24,64,256]{2,0,1:T(8,128)(2,1)S(1)}, u32[]{:S(2)}, u32[]{:S(2)}) async-start(bf16[24,64,256]{2,0,1:T(8,128)(2,1)} %broadcast_select_fusion), calls=%async_computation | async-start | bytes 1572864 | tf_op jit(solution)/shard_map/all_to_all | solution.py:89
  134.2 11.6 %copy-start.7 = (bf16[1,256,256]{2,1,0:T(8,128)(2,1)S(1)}, bf16[1,256,256]{2,1,0:T(8,128)(2,1)}, u32[]{:S(2)}) copy-start(bf16[1,256,256]{2,1,0:T(8,128)(2,1)} %param.23) | copy-start | bytes 393220
  135.6 32.2 %all-to-all-start.1 = ((bf16[64,2,3072]{2,1,0:T(2,128)(2,1)}), bf16[64,2,3072]{2,1,0:T(2,128)(2,1)}, u32[]{:S(2)}, u32[]{:S(2)}) async-start(bf16[64,2,3072]{2,1,0:T(2,128)(2,1)} %reshape.216), calls=%async_computation.1 | async-start | bytes 1572864 | tf_op jit(solution)/shard_map/all_to_all | solution.py:56
  145.0 141.6 %all-gather.9.cloned.1.call-start = ((), (), s32[]{:S(2)}) async-start(), calls=%async_computation.7 | async-start | bytes 2654208 | tf_op jit(solution)/shard_map/all_gather | solution.py:51
  167.8 32.0 %all-to-all-start.3 = ((bf16[64,2,3072]{2,1,0:T(2,128)(2,1)}), bf16[64,2,3072]{2,1,0:T(2,128)(2,1)}, u32[]{:S(2)}, u32[]{:S(2)}) async-start(bf16[64,2,3072]{2,1,0:T(2,128)(2,1)} %reshape.218), calls=%async_computation.3 | async-start | bytes 1572864 | tf_op jit(solution)/shard_map/all_to_all | solution.py:56
  183.5 8.6 %copy-start.8 = (bf16[4,64,64]{2,1,0:T(8,128)(2,1)S(1)}, bf16[4,64,64]{2,1,0:T(8,128)(2,1)}, u32[]{:S(2)}) copy-start(bf16[4,64,64]{2,1,0:T(8,128)(2,1)} %param.19) | copy-start | bytes 98308
  192.5 16.6 %copy-start.14 = (s32[8]{0:T(128)S(1)}, s32[8]{0:T(128)}, u32[]{:S(2)}) copy-start(s32[8]{0:T(128)} %param.15) | copy-start | bytes 100
  199.7 29.2 %all-to-all-start.2 = ((bf16[1,64,4,1536]{3,2,0,1:T(4,128)(2,1)}), bf16[1,64,4,1536]{3,2,0,1:T(4,128)(2,1)}, u32[]{:S(2)}, u32[]{:S(2)}) async-start(bf16[1,64,4,1536]{3,2,0,1:T(4,128)(2,1)} %copy.71), calls=%async_computation.2 | async-start | bytes 1572864 | tf_op jit(solution)/shard_map/all_to_all | solution.py:64
  215.0 8.6 %copy-start.9 = (bf16[4,64,64]{2,1,0:T(8,128)(2,1)S(1)}, bf16[4,64,64]{2,1,0:T(8,128)(2,1)}, u32[]{:S(2)}) copy-start(bf16[4,64,64]{2,1,0:T(8,128)(2,1)} %param.24) | copy-start | bytes 98308
  224.0 16.5 %copy-start.10 = (bf16[192,128]{1,0:T(8,128)(2,1)S(1)}, bf16[192,128]{1,0:T(8,128)(2,1)}, u32[]{:S(2)}) copy-start(bf16[192,128]{1,0:T(8,128)(2,1)} %param.22) | copy-start | bytes 147460
  229.0 71.7 %all-to-all-start.4 = ((bf16[1,64,4,1536]{3,2,0,1:T(4,128)(2,1)}), bf16[1,64,4,1536]{3,2,0,1:T(4,128)(2,1)}, u32[]{:S(2)}, u32[]{:S(2)}) async-start(bf16[1,64,4,1536]{3,2,0,1:T(4,128)(2,1)} %copy.79), calls=%async_computation.4 | async-start | bytes 1572864 | tf_op jit(solution)/shard_map/all_to_all | solution.py:64
  240.4 327.6 %all-reduce.2.cloned.1.call-start = ((), (), s32[]{:S(2)}) async-start(), calls=%async_computation.5 | async-start | bytes 196608 | tf_op jit(solution)/shard_map/psum | solution.py:106
  274.9 2.6 copy-start.3
  279.1 2.4 copy-start.2
  286.6 2.0 copy-start.4
  303.8 4.2 copy-start.11
  307.2 261.8 %copy-start.5 = (bf16[1536,128]{1,0:T(8,128)(2,1)S(1)}, bf16[1536,128]{1,0:T(8,128)(2,1)}, u32[]{:S(2)}) copy-start(bf16[1536,128]{1,0:T(8,128)(2,1)} %all-gather.1) | copy-start | bytes 1179652
  308.0 263.4 %copy-start.1 = (bf16[1,256,256]{2,1,0:T(8,128)(2,1)S(1)}, bf16[1,256,256]{2,1,0:T(8,128)(2,1)}, u32[]{:S(2)}) copy-start(bf16[1,256,256]{2,1,0:T(8,128)(2,1)} %param.18) | copy-start | bytes 393220
  322.6 248.0 %copy-start.15 = (s32[4]{0:T(128)S(1)}, s32[4]{0:T(128)}, u32[]{:S(2)}) copy-start(s32[4]{0:T(128)} %param.16) | copy-start | bytes 52
  (1 other events, 0.7 us)
Sparse Core Ops, SparseCore 0:
  10.1 46.8 all-gather.6
  147.9 60.3 all-gather.8
  308.1 259.8 all-reduce.1
where the time goes:
time: 587 us; the launch traced here: 578 us
  waiting for transfers between devices  288 us (49%)
  local copies, waits for them, and re-layouts  134 us (23%)
  starting transfers between devices  60.1 us (10%)
  blocking collectives  49 us (8%)
  other arithmetic  21.5 us (4%)
  between operations  14.4 us (2%)
  matrix products  10.7 us (2%)
    psum x1, waiting for transfers between devices, body(): totals = lax.psum(contribution, ('dp', 'ctx'))  244 us
    gather x2, local copies, waits for them, and re-layouts, body(): looked_up = jnp.take(embed_table, token_ids[0], axis=1)  63.1 us
    all_gather x2, blocking collectives, run_models(): lax.all_gather(head_stack, 'dp', axis=3, tiled=True)  49 us
    unnamed x42, local copies, waits for them, and re-layouts  23.9 us
    all_to_all x1, waiting for transfers between devices, body(): lax.all_to_all(looked_up, 'ctx', split_axis=1, concat_axis=0, tiled=True)  23.2 us
    all_to_all x2, starting transfers between devices, run_models(): lax.all_to_all(mixed_cols, 'ctx', split_axis=1, concat_axis=2, tiled=True)  20.8 us
    all_to_all x1, starting transfers between devices, body(): lax.all_to_all(looked_up, 'ctx', split_axis=1, concat_axis=0, tiled=True)  19.6 us
    all_to_all x2, starting transfers between devices, run_models(): lax.all_to_all(within, 'ctx', split_axis=2, concat_axis=1, tiled=True)  19.3 us
  transfers between devices with their start and end apart: 8, of which 5 were waited for; matrix products, arithmetic and copies ran while one was open for 27% of the time, Pallas kernels for 0%

commit v1 on v0

v1 whole, which is shorter than its diff:
```python
import functools
import jax
import jax.numpy as jnp
from jax import lax
from jax.experimental import pallas as pl
from jax.experimental.pallas import tpu as pltpu
from jax.sharding import PartitionSpec as P

MESH = pl.DeviceIdType.MESH
F32 = jnp.float32
BF16 = jnp.bfloat16
HALF_TILE = 4


def dot(a, b):
    return jnp.dot(a, b, preferred_element_type=F32)


def iota(shape, axis):
    return lax.broadcasted_iota(jnp.int32, shape, axis)


class Place:
    def __init__(self, n_d, n_c):
        self.n_d, self.n_c = n_d, n_c
        self.n_x = 4 if n_c == 64 else 1
        self.n_y = n_c // (2 * self.n_x)
        self.n_w = 2 * self.n_x
        self.z_lo_size = n_d // 2
        self.z_size = 2 * self.z_lo_size
        self.dp, self.ctx = lax.axis_index("dp"), lax.axis_index("ctx")
        self.y, self.w = self.ctx // self.n_w, lax.rem(self.ctx, self.n_w)
        self.z_hi, self.x = self.w // self.n_x, lax.rem(self.w, self.n_x)
        self.z_lo, self.core = self.dp // 2, lax.rem(self.dp, 2)
        self.z = self.z_hi * self.z_lo_size + self.z_lo

    def ctx_at(self, o):
        step_y = lax.rem(lax.rem(o, self.n_y) * 3, self.n_y)
        rest = o // self.n_y
        step_z, step_x = lax.rem(rest, 2), rest // 2
        y = lax.rem(self.y + step_y, self.n_y)
        z_hi = lax.rem(self.z_hi + step_z, 2)
        x = lax.rem(self.x + step_x, self.n_x)
        return y * self.n_w + z_hi * self.n_x + x

    def z_at(self, step):
        z = lax.rem(self.z + step, self.z_size)
        dp = lax.rem(z, self.z_lo_size) * 2 + self.core
        ctx = self.y * self.n_w + (z // self.z_lo_size) * self.n_x + self.x
        return dp, ctx

    def y_peer(self, o):
        return (self.dp, lax.rem(self.y + o, self.n_y) * self.n_w + self.w)

    def w_peer(self, o):
        return (self.dp, self.y * self.n_w + lax.rem(self.w + o, self.n_w))

    def d_peer(self, o):
        return (lax.rem(self.dp + o, self.n_d), self.ctx)


def remote(src, dst, send, recv, device):
    return pltpu.make_async_remote_copy(
        src_ref=src, dst_ref=dst, send_sem=send, recv_sem=recv,
        device_id=device, device_id_type=MESH)


def exchange(own, buf, send, recv, peer, me, count):
    copies = []
    for o in range(1, count):
        copy = remote(own, buf.at[me], send.at[o], recv.at[me], peer(o))
        copy.start()
        copies.append(copy)
    buf[me] = own[...]
    for o in range(1, count):
        slot = lax.rem(me + o, count)
        remote(own, buf.at[slot], send.at[o], recv.at[slot], peer(o)).wait_recv()
    return copies


def total_of(buf, count):
    total = buf[0]
    for j in range(1, count):
        total = total + buf[j]
    return total


def to_chunks(parts, ref):
    rows, width = parts[0].shape
    tiles = [p.reshape(rows // 8, 8, width) for p in parts]
    rolled = [pltpu.roll(t, HALF_TILE, 1) for t in tiles]
    upper = iota((1, 8, 1), 1) < HALF_TILE
    even = [jnp.where(upper, tiles[i], rolled[i + 1]) for i in (0, 2)]
    odd = [jnp.where(upper, rolled[i], tiles[i + 1]) for i in (0, 2)]
    ref[:, 0] = jnp.concatenate(even, axis=1).astype(BF16)
    ref[:, 1] = jnp.concatenate(odd, axis=1).astype(BF16)


def from_chunks(ref):
    even, odd = ref[:, 0].astype(F32), ref[:, 1].astype(F32)
    rows, width = even.shape[0] * 8, even.shape[2]
    upper = iota((1, 8, 1), 1) < HALF_TILE
    parts = []
    for i in (0, 1):
        e, o = even[:, 8 * i:8 * i + 8], odd[:, 8 * i:8 * i + 8]
        parts.append(jnp.where(upper, e, pltpu.roll(o, HALF_TILE, 1)).reshape(rows, width))
        parts.append(jnp.where(upper, pltpu.roll(e, HALF_TILE, 1), o).reshape(rows, width))
    return parts


def layer_kernel(
    dims, ids_ref, target_ref, table_ref, blocks_ref, across_ref, channel_ref, gain_ref, head_ref,
    out_ref, loss_ref,
    tall, x_send, x_recv, flipped, x_all, h_all, r_send, r_recv, s_send, s_recv,
    factors, gates, mix, spread, gather, padded, sums,
    buf_y, buf_w, buf_d, buf_l, own_y, own_w, own_l,
    x_sem, r_sem, s_sem, f_send, f_recv, g_send, g_recv, local_sem,
    send_y, recv_y, send_w, recv_w, send_d, recv_d, send_l, recv_l,
):
    n_d, n_c, seq_len = dims
    at = Place(n_d, n_c)
    feats, vocab = table_ref.shape
    block = blocks_ref.shape[1]
    half = block // 2
    width = channel_ref.shape[4]
    depth = channel_ref.shape[3]
    quarter = width // 4
    wide = gather.shape[0] // 4
    n_l = tall.shape[0] // feats
    n_z = at.z_size

    barrier = pltpu.get_barrier_semaphore()

    def greet(o, carry):
        pl.semaphore_signal(barrier, inc=1, device_id=(at.dp, at.ctx_at(o)), device_id_type=MESH)
        return carry

    lax.fori_loop(1, n_c, greet, 0)
    for o in range(1, n_d):
        pl.semaphore_signal(barrier, inc=1, device_id=at.d_peer(o), device_id_type=MESH)
    for step in (1, 2, n_z - 2, n_z - 1):
        pl.semaphore_signal(barrier, inc=1, device_id=at.z_at(step), device_id_type=MESH)

    def tall_pair(i, carry):
        start = pl.multiple_of(i * 2 * block, 2 * block)
        pair = table_ref[:, pl.ds(start, 2 * block)].astype(F32)
        tall[pl.ds(pl.multiple_of(i * 2 * feats, 2 * feats), 2 * feats), :] = jnp.concatenate(
            [pair[:, :block], pair[:, block:]], axis=0).astype(BF16)
        return carry

    full = vocab // (2 * block)
    lax.fori_loop(0, full, tall_pair, 0)
    if full * 2 < n_l:
        left = table_ref[:, full * 2 * block:].astype(F32)
        left = jnp.concatenate(
            [left, jnp.zeros((feats, 2 * block - left.shape[1]), F32)], axis=1)
        tall[full * 2 * feats:, :] = jnp.concatenate(
            [left[:, :block], left[:, block:]], axis=0).astype(BF16)

    pl.semaphore_wait(barrier, n_c - 1 + n_d - 1 + 4)

    def shard(m, dp):
        return factors.at[m, :, :, pl.ds(pl.multiple_of(dp * depth, depth), depth), :]

    steps = (1, n_z - 1, lax.rem(2 + at.core * (n_z - 4), n_z))
    sources = []
    for step in steps:
        sources.append(at.z_at(n_z - step)[0])
    pending = []
    for m in range(2):
        for j, step in enumerate(steps):
            copy = remote(channel_ref.at[m], shard(m, at.dp), f_send.at[m, j], f_recv.at[m, j],
                          at.z_at(step))
            copy.start()
            pending.append(copy)
    own_factors = []
    for m in range(2):
        copy = pltpu.make_async_copy(channel_ref.at[m], shard(m, at.dp), local_sem.at[m])
        copy.start()
        own_factors.append(copy)

    def lookup(i, carry):
        dest = at.ctx_at(n_c - 1 - i)
        ids = ids_ref[pl.ds(dest, 1), :]
        low, high = lax.rem(ids, block), ids // block
        hot = jnp.where(iota((block, block), 0) == low, 1.0, 0.0).astype(BF16)
        found = jnp.zeros((feats, block), F32)
        picked = dot(tall[...], hot)
        for l in range(n_l):
            found = jnp.where(high == l, picked[l * feats:(l + 1) * feats], found)
        x_send[dest] = jnp.concatenate([found[:, :half], found[:, half:]], axis=0).astype(BF16)

        @pl.when(i < n_c - 1)
        def _():
            remote(x_send.at[dest], x_recv.at[at.ctx], x_sem.at[0], x_sem.at[1],
                   (at.dp, dest)).start()

        @pl.when(i == n_c - 1)
        def _():
            pltpu.make_async_copy(x_send.at[dest], x_recv.at[at.ctx], x_sem.at[1]).start()

        return carry

    lax.fori_loop(0, n_c, lookup, 0)

    sibling = (at.dp + 1 - 2 * at.core, at.ctx)
    other = at.dp + 1 - 2 * at.core
    for m in range(2):
        own_factors[m].wait()
        for j, source in enumerate([at.dp] + sources):
            if j:
                remote(channel_ref.at[m], shard(m, source), f_send.at[m, j - 1],
                       f_recv.at[m, j - 1], sibling).wait_recv()
            copy = remote(shard(m, source), shard(m, source), g_send.at[m, j], g_recv.at[m, j],
                          sibling)
            copy.start()
            pending.append(copy)

    group = across_ref.shape[1]
    tall_one = jnp.where(iota((block, n_c), 0) // group == iota((block, n_c), 1), 1.0, 0.0)
    wide_one = jnp.where(iota((n_c, block), 1) // group == iota((n_c, block), 0), 1.0, 0.0)
    row_b, col_b = lax.rem(iota((block, block), 0), group), lax.rem(iota((block, block), 1), group)
    for m in range(2):
        total = jnp.zeros((block, block), F32)
        for b in range(group):
            piece = dot(dot(tall_one.astype(BF16), across_ref[m, b]).astype(BF16),
                        wide_one.astype(BF16))
            total = jnp.where((row_b == b) & (col_b == b), piece, total)
        mix[m] = total.astype(BF16)
    place, lane = iota((width, 4 * wide), 0), iota((width, 4 * wide), 1)
    inner = lax.rem(lane, wide)
    spread[...] = jnp.where(
        (place == (lane // wide) * quarter + inner) & (inner < quarter), 1.0, 0.0).astype(BF16)
    place, lane = iota((4 * wide, width), 0), iota((4 * wide, width), 1)
    inner = lax.rem(place, wide)
    gather[...] = jnp.where(
        (lane == inner * 4 + place // wide) & (inner < quarter), 1.0, 0.0).astype(BF16)

    def all_sent(buf, sem):
        if len(buf.shape) == 3:
            view = buf.at[pl.ds(0, n_c - 1)]
            pltpu.make_async_copy(view, view, sem).wait()
        else:
            view = buf.at[pl.ds(0, n_c // 2 - 1)]
            pltpu.make_async_copy(view, view, sem).wait()
            view = buf.at[0, 0]
            pltpu.make_async_copy(view, view, sem).wait()

    def send_all(send, recv, sems):
        def one(i, carry):
            dest = at.ctx_at(n_c - 1 - i)
            remote(send.at[dest // 2, lax.rem(dest, 2)],
                   recv.at[at.ctx // 2, lax.rem(at.ctx, 2)],
                   sems.at[0], sems.at[1], (at.dp, dest)).start()
            return carry

        lax.fori_loop(0, n_c - 1, one, 0)
        pltpu.make_async_copy(send.at[at.ctx // 2, lax.rem(at.ctx, 2)],
                              recv.at[at.ctx // 2, lax.rem(at.ctx, 2)], sems.at[1]).start()

    pltpu.make_async_copy(x_recv, x_recv, x_sem.at[1]).wait()

    def flip(i, carry):
        both = x_recv[i].astype(F32)
        start = pl.multiple_of(i * feats, feats)
        flipped[0, pl.ds(start, feats), :] = both[:feats]
        flipped[1, pl.ds(start, feats), :] = both[feats:]
        return carry

    lax.fori_loop(0, n_c, flip, 0)
    squares = []
    for i in range(2):
        square = jnp.zeros((half, 1), F32)
        for k in range(4):
            values = flipped[i, k * width:(k + 1) * width, :].T
            square = square + jnp.sum(values * values, axis=1, keepdims=True)
            x_all[k, i * half:(i + 1) * half, :] = values
        squares.append(square)
    scale = lax.rsqrt(jnp.concatenate(squares, axis=0) / (4 * width) + 1e-06)

    for m in range(2):
        parts = []
        for k in range(4):
            gain = gain_ref[m:m + 1, k * width:(k + 1) * width].astype(F32)
            h = (x_all[k] * scale * gain).astype(BF16)
            h_all[m, k] = h
            parts.append(dot(blocks_ref[m], h))
        to_chunks(parts, r_send.at[m])
        send_all(r_send.at[m], r_recv.at[m], r_sem.at[m])

    def gate(m):
        for j in range(4):
            source = (at.dp if j == 0 else sources[j - 1]) + 1 - 2 * at.core
            remote(shard(m, source), shard(m, source), g_send.at[m, j], g_recv.at[m, j],
                   sibling).wait_recv()
        for k in range(4):
            first = dot(h_all[m, k], factors[m, 0, k]).astype(BF16)
            first = dot(first, spread[...]).astype(BF16)
            for q in range(4):
                padded[q, :, k * wide:(k + 1) * wide] = first[:, q * wide:(q + 1) * wide]
        for q in range(4):
            second = dot(gather[...], factors[m, 1, q]).astype(BF16)
            z = dot(padded[q], second)
            gates[m, q] = 1.0 / (1.0 + jnp.exp(-z))

    gate(0)
    for m in range(2):
        pltpu.make_async_copy(r_recv.at[m], r_recv.at[m], r_sem.at[m, 1]).wait()
        parts = from_chunks(r_recv.at[m])
        to_chunks([dot(mix[m], part.astype(BF16)) for part in parts], s_send.at[m])
        send_all(s_send.at[m], s_recv.at[m], s_sem.at[m])
    gate(1)
    for m in range(2):
        pltpu.make_async_copy(s_recv.at[m], s_recv.at[m], s_sem.at[m, 1]).wait()
        parts = from_chunks(s_recv.at[m])
        for k in range(4):
            y = (x_all[k] + parts[k] * gates[m, k]).astype(BF16)
            if m == 0:
                out_ref[:, k * width:(k + 1) * width] = y
            sums[m * 4 + k:m * 4 + k + 1, :] = jnp.sum(y.astype(F32), axis=0, keepdims=True)

    pending += exchange(sums, buf_y, send_y, recv_y, at.y_peer, at.y, at.n_y)
    own_y[...] = total_of(buf_y, at.n_y)
    pending += exchange(own_y, buf_w, send_w, recv_w, at.w_peer, at.w, at.n_w)
    own_w[...] = total_of(buf_w, at.n_w) / seq_len
    pending += exchange(own_w, buf_d, send_d, recv_d, at.d_peer, at.dp, n_d)
    local = []
    for m in range(2):
        mine = (iota((8, 1), 0) == m * 4 + at.dp * 4 // n_d).astype(F32)
        model = (iota((8, 1), 0) // 4 == m).astype(F32)
        rows, norms = [], []
        for n in range(n_d):
            pooled = buf_d[n]
            rows.append(jnp.sum(pooled * mine, axis=0, keepdims=True))
            square = jnp.sum(pooled * pooled * model, axis=0, keepdims=True)
            norms.append(jnp.sum(square, axis=1, keepdims=True))
        norm = lax.rsqrt(jnp.concatenate(norms, axis=0) / (4 * width) + 1e-06)
        local.append(jnp.dot(jnp.concatenate(rows, axis=0) * norm, head_ref[m],
                             precision=lax.Precision.HIGHEST, preferred_element_type=F32))
    own_l[...] = jnp.concatenate(local, axis=1)
    pending += exchange(own_l, buf_l, send_l, recv_l, at.d_peer, at.dp, n_d)
    logits = total_of(buf_l, n_d)
    classes = logits.shape[1] // 2
    chosen = iota((n_d, classes), 1) == target_ref[...]
    losses = []
    for part in (logits[:, :classes], logits[:, classes:]):
        top = jnp.max(part, axis=1, keepdims=True)
        summed = jnp.log(jnp.sum(jnp.exp(part - top), axis=1, keepdims=True)) + top
        losses.append(summed - jnp.sum(jnp.where(chosen, part, 0.0), axis=1, keepdims=True))
    loss_ref[...] = jnp.broadcast_to(losses[0] - losses[1], loss_ref.shape)

    all_sent(x_send, x_sem.at[0])
    for m in range(2):
        all_sent(r_send.at[m], r_sem.at[m, 0])
        all_sent(s_send.at[m], s_sem.at[m, 0])
    for copy in pending:
        copy.wait_send()


def layer_call(ids, target, table, blocks, across, channel, gain, head, seq_len):
    n_d, n_c = lax.axis_size("dp"), lax.axis_size("ctx")
    n_w = 8 if n_c == 64 else 2
    n_y = n_c // n_w
    feats, vocab = table.shape
    block = blocks.shape[1]
    width, depth = channel.shape[4], channel.shape[3]
    wide = -(-(width // 4) // 128) * 128
    n_l = -(-vocab // (2 * block)) * 2
    classes = head.shape[2]
    dma = pltpu.SemaphoreType.DMA
    chunks = (2, n_c // 2, 2, 16, width)
    return pl.pallas_call(
        functools.partial(layer_kernel, (n_d, n_c, seq_len)),
        out_shape=(jax.ShapeDtypeStruct((block, 4 * width), BF16),
                   jax.ShapeDtypeStruct((n_d, 128), F32)),
        in_specs=[pl.BlockSpec(memory_space=pltpu.VMEM)] * 8,
        out_specs=(pl.BlockSpec(memory_space=pltpu.VMEM), pl.BlockSpec(memory_space=pltpu.VMEM)),
        scratch_shapes=[
            pltpu.VMEM((n_l * feats, block), BF16),
            pltpu.VMEM((n_c, 2 * feats, block // 2), BF16),
            pltpu.VMEM((n_c, 2 * feats, block // 2), BF16),
            pltpu.VMEM((2, n_c * feats, block // 2), F32),
            pltpu.VMEM((4, block, width), F32),
            pltpu.VMEM((2, 4, block, width), BF16),
            pltpu.VMEM(chunks, BF16), pltpu.VMEM(chunks, BF16),
            pltpu.VMEM(chunks, BF16), pltpu.VMEM(chunks, BF16),
            pltpu.VMEM((2, 2, 4, depth * n_d, width), BF16),
            pltpu.VMEM((2, 4, block, width), F32),
            pltpu.VMEM((2, block, block), BF16),
            pltpu.VMEM((width, 4 * wide), BF16), pltpu.VMEM((4 * wide, width), BF16),
            pltpu.VMEM((4, block, 4 * wide), BF16),
            pltpu.VMEM((8, width), F32),
            pltpu.VMEM((n_y, 8, width), F32), pltpu.VMEM((n_w, 8, width), F32),
            pltpu.VMEM((n_d, 8, width), F32), pltpu.VMEM((n_d, n_d, 2 * classes), F32),
            pltpu.VMEM((8, width), F32), pltpu.VMEM((8, width), F32),
            pltpu.VMEM((n_d, 2 * classes), F32),
            dma((2,)), dma((2, 2)), dma((2, 2)),
            dma((2, 3)), dma((2, 3)), dma((2, 4)), dma((2, 4)), dma((2,)),
            dma((n_y,)), dma((n_y,)), dma((n_w,)), dma((n_w,)),
            dma((n_d,)), dma((n_d,)), dma((n_d,)), dma((n_d,)),
        ],
        compiler_params=pltpu.CompilerParams(
            collective_id=1, has_side_effects=True, vmem_limit_bytes=56 * 1024 * 1024),
        name="layer",
    )(ids, target, table, blocks, across, channel, gain, head)


def body(
    token_ids,
    target_ids,
    candidates,
    embed_table,
    online_blocks,
    online_across,
    online_channel,
    online_gain,
    online_head,
    ref_blocks,
    ref_across,
    ref_channel,
    ref_gain,
    ref_head,
):
    n_d, n_c = lax.axis_size("dp"), lax.axis_size("ctx")
    seq_len = token_ids.shape[1]
    heads = jnp.stack([online_head, ref_head]).astype(F32)
    part = heads.shape[1]
    reps = n_d // 4
    slot = lax.rem(lax.axis_index("dp"), reps)
    rows = jnp.arange(part * reps, dtype=jnp.int32) // part
    head = jnp.where((rows == slot)[None, :, None], jnp.concatenate([heads] * reps, axis=1), 0.0)
    out, loss = layer_call(
        token_ids.reshape(n_c, seq_len // n_c),
        target_ids.reshape(n_d, 1),
        embed_table,
        jnp.concatenate([online_blocks, ref_blocks]),
        jnp.stack([online_across, ref_across]),
        jnp.stack([online_channel, ref_channel]),
        jnp.stack([online_gain, ref_gain]),
        head,
        seq_len,
    )
    scores = loss[:, 0]
    pick_mask = (candidates[:, None] == jnp.arange(n_d, dtype=jnp.int32)[None]).astype(F32)
    picked = jnp.sum(pick_mask * scores[None], axis=1)
    return (out, scores, picked)


def solution(mesh):
    in_specs = (
        P("dp", None),
        P(),
        P(),
        P("ctx", None),
        P("ctx", None, None),
        P("ctx", None, None),
        P(None, None, "dp", None),
        P(),
        P("dp", None),
        P("ctx", None, None),
        P("ctx", None, None),
        P(None, None, "dp", None),
        P(),
        P("dp", None),
    )
    out_specs = (P(("dp", "ctx"), None), P(), P())
    return jax.shard_map(body, mesh=mesh, in_specs=in_specs, out_specs=out_specs, check_vma=False)
```

time: 587 us -> 184 us (0.31); the launches traced: 578 us -> 183 us
  waiting for transfers between devices: 288 us -> 0 us
  Pallas kernels: 0 us -> 167 us
  local copies, waits for them, and re-layouts: 134 us -> 6.79 us
  starting transfers between devices: 60.1 us -> 0 us
  blocking collectives: 49 us -> 0 us
  between operations: 14.4 us -> 0.68 us
  other arithmetic: 21.5 us -> 8.82 us
  matrix products: 10.7 us -> 0 us
    psum x1 -> x0, waiting for transfers between devices: 244 us -> none  [body(): totals = lax.psum(contribution, ('dp', 'ctx'))]
    pallas_call x0 -> x1, Pallas kernels: none -> 167 us  [layer_call(): pl.pallas_call(functools.partial(layer_kernel, (n_d, n_c, seq_len)), out_...]
    gather x2 -> x0, local copies, waits for them, and re-layouts: 63.1 us -> none  [body(): looked_up = jnp.take(embed_table, token_ids[0], axis=1)]
    all_to_all x5 -> x0, starting transfers between devices: 59.7 us -> none  [the longest x2 20.8 us: run_models(): lax.all_to_all(mixed_cols, 'ctx', split_axis=1, concat_axis=2, tiled=True)]
    all_gather x2 -> x0, blocking collectives: 49 us -> none  [run_models(): lax.all_gather(head_stack, 'dp', axis=3, tiled=True)]
    all_to_all x5 -> x0, waiting for transfers between devices: 43.1 us -> none  [the longest x1 23.2 us: body(): lax.all_to_all(looked_up, 'ctx', split_axis=1, concat_axis=0, tiled=True)]
    unnamed x42 -> x10, local copies, waits for them, and re-layouts: 23.9 us -> 2.59 us
    all_to_all x2 -> x0, local copies, waits for them, and re-layouts: 13.8 us -> none  [run_models(): lax.all_to_all(within, 'ctx', split_axis=2, concat_axis=1, tiled=True)]
  transfers between devices with their start and end apart: 8 -> 0, of which waited for: 5 -> 0; matrix products, arithmetic and copies ran while one was open for 27% -> 0% of each run, Pallas kernels for 0% -> 0%
where the time goes in v1:
time: 184 us; the launch traced here: 183 us
  Pallas kernels  167 us (91%)
  other arithmetic  8.82 us (5%)
  local copies, waits for them, and re-layouts  6.79 us (4%)
    pallas_call x1, Pallas kernels, layer_call(): pl.pallas_call(functools.partial(layer_kernel, (n_d, n_c, seq_len)), out_...  167 us

profile of v1, /device:TPU:1, one launch (start us, length us, event | category | flops | bytes accessed | tf_op | source)
XLA Modules:
  0.0 183.2 jit_solution(12116486102029483049)
XLA Ops:
  0.6 0.0 copy-start
  0.6 0.0 copy-start.1
  0.7 1.4 copy.19.target_ref
  2.1 0.7 stack.42
  2.7 0.7 stack.43
  3.4 0.6 pad_maximum_fusion.3.gain_ref
  4.0 0.5 broadcast.36
  4.6 1.6 reduce.5
  6.2 0.6 reshape.28.ids_ref
  6.8 1.6 pad_maximum_fusion.2.across_ref
  8.4 1.7 pad_maximum_fusion.1.blocks_ref
  10.1 1.7 convert_select_fusion.head_ref
  11.8 0.0 copy-done
  11.8 0.0 copy-done.1
  11.8 0.9 pad_maximum_fusion.channel_ref
  12.7 0.0 copy-start.3
  12.7 167.0 %layer.1 = (bf16[256,1536]{1,0:T(8,128)(2,1)}, f32[8,128]{1,0:T(8,128)}) custom-call(s32[64,256]{1,0:T(8,128)} %reshape.28.ids_ref, s32[8,1]{1,0:T(8,128)} %copy.19.target_ref, bf16[24,30528]{1,0:T(8,128)(2,1)} %table_ref.1, bf16[2,256,256]{2,1,0:T(8,128)(2,1)} %pad_maximum_fusion.1.blocks_ref, bf16[2,4,64,64]{3,2,1,0:T(8,128)(2,1)} %pad_maximum_fusion.2.across_ref, ...), custom_call_target="tpu_custom_call" | custom-call | tf_op jit(solution)/shard_map/layer/pallas_call | solution.py:372
  179.7 0.8 slice_reduce_fusion
  180.5 0.0 copy-done.3
  180.5 0.0 copy-start.2
  180.5 0.7 select_reduce_fusion
  181.2 2.1 %copy.21 = bf16[256,1536]{1,0:T(8,128)(2,1)} copy(bf16[256,1536]{1,0:T(8,128)(2,1)} %get-tuple-element.10) | data formatting | bytes 1572864
  183.2 0.0 copy-done.2
  (1 shorter events, 0.0 us)
Async XLA Ops:
  0.6 11.2 %copy-start = (bf16[2,4,48,384]{3,2,1,0:T(8,128)(2,1)S(1)}, bf16[2,4,48,384]{3,2,1,0:T(8,128)(2,1)}, u32[]{:S(2)}) copy-start(bf16[2,4,48,384]{3,2,1,0:T(8,128)(2,1)} %param.25) | copy-start | bytes 884740
  0.6 11.2 %copy-start.1 = (bf16[2,4,48,384]{3,2,1,0:T(8,128)(2,1)S(1)}, bf16[2,4,48,384]{3,2,1,0:T(8,128)(2,1)}, u32[]{:S(2)}) copy-start(bf16[2,4,48,384]{3,2,1,0:T(8,128)(2,1)} %param.20) | copy-start | bytes 884740
  12.7 167.8 %copy-start.3 = (s32[4]{0:T(128)S(1)}, s32[4]{0:T(128)}, u32[]{:S(2)}) copy-start(s32[4]{0:T(128)} %param.16) | copy-start | bytes 52
  180.5 2.8 %copy-start.2 = (f32[8]{0:T(128)}, f32[8]{0:T(128)S(1)}, u32[]{:S(2)}) copy-start(f32[8]{0:T(128)S(1)} %slice_reduce_fusion) | copy-start | bytes 100

commit v2 on v1

v2 whole, which is shorter than its diff:
```python
import functools
import jax
import jax.numpy as jnp
from jax import lax
from jax.experimental import pallas as pl
from jax.experimental.pallas import tpu as pltpu
from jax.sharding import PartitionSpec as P

MESH = pl.DeviceIdType.MESH
F32 = jnp.float32
BF16 = jnp.bfloat16
HALF_TILE = 4


def dot(a, b):
    return jnp.dot(a, b, preferred_element_type=F32)


def iota(shape, axis):
    return lax.broadcasted_iota(jnp.int32, shape, axis)


class Place:
    def __init__(self, n_d, n_c):
        self.n_d, self.n_c = n_d, n_c
        self.n_x = 4 if n_c == 64 else n_c // 2
        self.n_y = n_c // (2 * self.n_x)
        self.n_w = 2 * self.n_x
        self.z_lo_size = n_d // 2
        self.z_size = 2 * self.z_lo_size
        self.dp, self.ctx = lax.axis_index("dp"), lax.axis_index("ctx")
        self.y, self.w = self.ctx // self.n_w, lax.rem(self.ctx, self.n_w)
        self.z_hi, self.x = self.w // self.n_x, lax.rem(self.w, self.n_x)
        self.z_lo, self.core = self.dp // 2, lax.rem(self.dp, 2)
        self.z = self.z_hi * self.z_lo_size + self.z_lo

    def ctx_at(self, o):
        step_y = lax.rem(lax.rem(o, self.n_y) * 3, self.n_y)
        rest = o // self.n_y
        step_z, step_x = lax.rem(rest, 2), rest // 2
        y = lax.rem(self.y + step_y, self.n_y)
        z_hi = lax.rem(self.z_hi + step_z, 2)
        x = lax.rem(self.x + step_x, self.n_x)
        return y * self.n_w + z_hi * self.n_x + x

    def z_at(self, step):
        z = lax.rem(self.z + step, self.z_size)
        dp = lax.rem(z, self.z_lo_size) * 2 + self.core
        ctx = self.y * self.n_w + (z // self.z_lo_size) * self.n_x + self.x
        return dp, ctx

    def x_peer(self, o):
        x = lax.rem(self.x + o, self.n_x)
        return (self.dp, self.y * self.n_w + self.z_hi * self.n_x + x)

    def y_peer(self, o):
        return (self.dp, lax.rem(self.y + o, self.n_y) * self.n_w + self.w)

    def w_peer(self, o):
        return (self.dp, self.y * self.n_w + lax.rem(self.w + o, self.n_w))

    def d_peer(self, o):
        return (lax.rem(self.dp + o, self.n_d), self.ctx)


def remote(src, dst, send, recv, device):
    return pltpu.make_async_remote_copy(
        src_ref=src, dst_ref=dst, send_sem=send, recv_sem=recv,
        device_id=device, device_id_type=MESH)


def spread_out(own, buf, send, recv, peer, me, count):
    copies = []
    for o in range(1, count):
        copy = remote(own, buf.at[me], send.at[o], recv.at[me], peer(o))
        copy.start()
        copies.append(copy)
    buf[me] = own[...]
    return copies


def gathered(own, buf, send, recv, peer, me, count):
    for o in range(1, count):
        slot = lax.rem(me + o, count)
        remote(own, buf.at[slot], send.at[o], recv.at[slot], peer(o)).wait_recv()


def total_of(buf, count):
    total = buf[0]
    for j in range(1, count):
        total = total + buf[j]
    return total


def to_chunks(parts, ref):
    rows, width = parts[0].shape
    tiles = [p.reshape(rows // 8, 8, width) for p in parts]
    rolled = [pltpu.roll(t, HALF_TILE, 1) for t in tiles]
    upper = iota((1, 8, 1), 1) < HALF_TILE
    even = [jnp.where(upper, tiles[i], rolled[i + 1]) for i in (0, 2)]
    odd = [jnp.where(upper, rolled[i], tiles[i + 1]) for i in (0, 2)]
    ref[:, 0] = jnp.concatenate(even, axis=1).astype(BF16)
    ref[:, 1] = jnp.concatenate(odd, axis=1).astype(BF16)


def from_chunks(ref):
    even, odd = ref[:, 0].astype(F32), ref[:, 1].astype(F32)
    rows, width = even.shape[0] * 8, even.shape[2]
    upper = iota((1, 8, 1), 1) < HALF_TILE
    parts = []
    for i in (0, 1):
        e, o = even[:, 8 * i:8 * i + 8], odd[:, 8 * i:8 * i + 8]
        parts.append(jnp.where(upper, e, pltpu.roll(o, HALF_TILE, 1)).reshape(rows, width))
        parts.append(jnp.where(upper, pltpu.roll(e, HALF_TILE, 1), o).reshape(rows, width))
    return parts


def layer_kernel(
    dims, ids_ref, target_ref, candidate_ref, table_ref,
    online_blocks, online_across, online_channel, online_gain, online_head,
    frozen_blocks, frozen_across, frozen_channel, frozen_gain, frozen_head,
    out_ref, score_ref,
    tall, xa_send, xa_recv, xb_send, xb_recv, flipped, x_all, r_send, r_recv, y_send, y_recv,
    factors, gates, mix, spread, gather, padded, sums,
    buf_y, buf_w, buf_d, buf_l, own_y, own_w, own_l,
    xa_sem, xb_sem, r_sem, y_sem, f_send, f_recv, e_send, e_recv, g_send, g_recv, local_sem,
    send_y, recv_y, send_w, recv_w, send_d, recv_d, send_l, recv_l,
):
    n_d, n_c, seq_len = dims
    at = Place(n_d, n_c)
    blocks_refs = (online_blocks, frozen_blocks)
    across_refs = (online_across, frozen_across)
    channel_refs = (online_channel, frozen_channel)
    gain_refs = (online_gain, frozen_gain)
    head_refs = (online_head, frozen_head)
    feats, vocab = table_ref.shape
    block = online_blocks.shape[1]
    half = block // 2
    depth, width = online_channel.shape[2:]
    quarter = width // 4
    wide = gather.shape[0] // 4
    n_l = tall.shape[0] // feats
    n_z = at.z_size
    group = online_across.shape[0]

    barrier = pltpu.get_barrier_semaphore()

    def greet(o, carry):
        pl.semaphore_signal(barrier, inc=1, device_id=(at.dp, at.ctx_at(o)), device_id_type=MESH)
        return carry

    lax.fori_loop(1, n_c, greet, 0)
    for o in range(1, n_d):
        pl.semaphore_signal(barrier, inc=1, device_id=at.d_peer(o), device_id_type=MESH)
    for step in (1, 2, n_z - 2, n_z - 1):
        pl.semaphore_signal(barrier, inc=1, device_id=at.z_at(step), device_id_type=MESH)

    def tall_pair(i, carry):
        start = pl.multiple_of(i * 2 * block, 2 * block)
        pair = table_ref[:, pl.ds(start, 2 * block)].astype(F32)
        tall[pl.ds(pl.multiple_of(i * 2 * feats, 2 * feats), 2 * feats), :] = jnp.concatenate(
            [pair[:, :block], pair[:, block:]], axis=0).astype(BF16)
        return carry

    full = vocab // (2 * block)
    lax.fori_loop(0, full, tall_pair, 0)
    if full * 2 < n_l:
        left = table_ref[:, full * 2 * block:].astype(F32)
        left = jnp.concatenate(
            [left, jnp.zeros((feats, 2 * block - left.shape[1]), F32)], axis=1)
        tall[full * 2 * feats:, :] = jnp.concatenate(
            [left[:, :block], left[:, block:]], axis=0).astype(BF16)

    pl.semaphore_wait(barrier, n_c - 1 + n_d - 1 + 4)

    n_k = 4 // at.n_x

    def shard(m, dp, x=None):
        rows = pl.ds(pl.multiple_of(dp * depth, depth), depth)
        if x is None:
            return factors.at[m, :, :, rows, :]
        return factors.at[m, :, pl.ds(x * n_k, n_k), rows, :]

    steps = (1, n_z - 1, lax.rem(2 + at.core * (n_z - 4), n_z))
    sources = [at.z_at(n_z - step)[0] for step in steps]
    pending = []
    for m in range(2):
        for j, step in enumerate(steps):
            copy = remote(channel_refs[m].at[:, pl.ds(at.x * n_k, n_k)], shard(m, at.dp, at.x),
                          f_send.at[m, j], f_recv.at[m, j], at.z_at(step))
            copy.start()
            pending.append(copy)
    own_factors = []
    for m in range(2):
        copy = pltpu.make_async_copy(channel_refs[m], shard(m, at.dp), local_sem.at[m])
        copy.start()
        own_factors.append(copy)

    def send_found(low, high, i, dest, send, recv, sems):
        hot = jnp.where(iota((block, block), 0).astype(F32) == low, 1.0, 0.0).astype(BF16)
        found = jnp.zeros((feats, block), F32)
        picked = dot(tall[...], hot)
        for l in range(n_l):
            found = jnp.where(high == float(l), picked[l * feats:(l + 1) * feats], found)
        send[dest] = jnp.concatenate([found[:, :half], found[:, half:]], axis=0).astype(BF16)

        @pl.when(i < n_c - 1)
        def _():
            remote(send.at[dest], recv.at[at.ctx], sems.at[0], sems.at[1], (at.dp, dest)).start()

        @pl.when(i == n_c - 1)
        def _():
            pltpu.make_async_copy(send.at[dest], recv.at[at.ctx], sems.at[1]).start()

    def lookup_own(i, carry):
        dest = at.ctx_at(n_c - 1 - i)
        ids = ids_ref[pl.ds(dest, 1), :]
        low, high = lax.rem(ids, block).astype(F32), (ids // block).astype(F32)
        send_found(low, high, i, dest, xa_send, xa_recv, xa_sem)
        return carry

    def lookup_across(i, carry):
        dest = at.ctx_at(n_c - 1 - i)
        ids = ids_ref[...]
        both = jnp.concatenate([lax.rem(ids, block), ids // block], axis=0)
        offset = lax.rem(iota((block, block), 1), group) + dest * group
        pick = jnp.where(iota((block, block), 0) == offset, 1.0, 0.0).astype(BF16)
        both = dot(both.astype(F32).astype(BF16), pick)
        mine = iota((n_c, block), 1) // group == iota((n_c, block), 0)
        low = jnp.sum(jnp.where(mine, both[:n_c], 0.0), axis=0, keepdims=True)
        high = jnp.sum(jnp.where(mine, both[n_c:], 0.0), axis=0, keepdims=True)
        send_found(low, high, i, dest, xb_send, xb_recv, xb_sem)
        return carry

    def unpack(recv, sems):
        pltpu.make_async_copy(recv, recv, sems.at[1]).wait()

        def flip(i, carry):
            both = recv[i].astype(F32)
            start = pl.multiple_of(i * feats, feats)
            flipped[0, pl.ds(start, feats), :] = both[:feats]
            flipped[1, pl.ds(start, feats), :] = both[feats:]
            return carry

        lax.fori_loop(0, n_c, flip, 0)
        squares = []
        for i in range(2):
            square = jnp.zeros((half, 1), F32)
            for k in range(4):
                values = flipped[i, k * width:(k + 1) * width, :].T
                square = square + jnp.sum(values * values, axis=1, keepdims=True)
                x_all[k, i * half:(i + 1) * half, :] = values
            squares.append(square)
        return lax.rsqrt(jnp.concatenate(squares, axis=0) / (4 * width) + 1e-06)

    def normed(m, k, scale):
        gain = gain_refs[m][:, k * width:(k + 1) * width].astype(F32)
        return (x_all[k] * scale * gain).astype(BF16)

    def send_part(send, recv, sems, first, last):
        def one(i, carry):
            dest = at.ctx_at(n_c - 1 - i)
            remote(send.at[dest // 2, lax.rem(dest, 2)],
                   recv.at[at.ctx // 2, lax.rem(at.ctx, 2)],
                   sems.at[0], sems.at[1], (at.dp, dest)).start()
            return carry

        lax.fori_loop(first, last, one, 0)

    def keep_own(send, recv, sems):
        pltpu.make_async_copy(send.at[at.ctx // 2, lax.rem(at.ctx, 2)],
                              recv.at[at.ctx // 2, lax.rem(at.ctx, 2)], sems.at[1]).start()

    def within(m, scale):
        to_chunks([dot(blocks_refs[m][0], normed(m, k, scale)) for k in range(4)], r_send.at[m])
        send_part(r_send.at[m], r_recv.at[m], r_sem.at[m], 0, n_c - 1)
        keep_own(r_send.at[m], r_recv.at[m], r_sem.at[m])

    lax.fori_loop(0, n_c, lookup_own, 0)

    for m in range(2):
        for j, source in enumerate(sources):
            remote(shard(m, source, at.x), shard(m, source, at.x), f_send.at[m, j],
                   f_recv.at[m, j], at.z_at(steps[j])).wait_recv()
            for o in range(1, at.n_x):
                copy = remote(shard(m, source, at.x), shard(m, source, at.x),
                              e_send.at[m, j, o - 1], e_recv.at[m, j, o - 1], at.x_peer(o))
                copy.start()
                pending.append(copy)

    scale = unpack(xa_recv, xa_sem)
    within(0, scale)
    lax.fori_loop(0, n_c, lookup_across, 0)
    within(1, scale)

    other = at.dp + 1 - 2 * at.core
    sibling = (other, at.ctx)
    for m in range(2):
        own_factors[m].wait()
        for j, source in enumerate([at.dp] + sources):
            if j:
                for o in range(1, at.n_x):
                    part = shard(m, source, lax.rem(at.x + at.n_x - o, at.n_x))
                    remote(part, part, e_send.at[m, j - 1, o - 1], e_recv.at[m, j - 1, o - 1],
                           at.x_peer(o)).wait_recv()
            copy = remote(shard(m, source), shard(m, source), g_send.at[m, j], g_recv.at[m, j],
                          sibling)
            copy.start()
            pending.append(copy)

    tall_one = jnp.where(iota((block, n_c), 0) // group == iota((block, n_c), 1), 1.0, 0.0)
    wide_one = jnp.where(iota((n_c, block), 1) // group == iota((n_c, block), 0), 1.0, 0.0)
    row_b, col_b = lax.rem(iota((block, block), 0), group), lax.rem(iota((block, block), 1), group)
    for m in range(2):
        total = jnp.zeros((block, block), F32)
        for b in range(group):
            piece = dot(dot(tall_one.astype(BF16), across_refs[m][b]).astype(BF16),
                        wide_one.astype(BF16))
            total = jnp.where((row_b == b) & (col_b == b), piece, total)
        mix[m] = total.astype(BF16)
    place, lane = iota((width, 4 * wide), 0), iota((width, 4 * wide), 1)
    inner = lax.rem(lane, wide)
    spread[...] = jnp.where(
        (place == (lane // wide) * quarter + inner) & (inner < quarter), 1.0, 0.0).astype(BF16)
    place, lane = iota((4 * wide, width), 0), iota((4 * wide, width), 1)
    inner = lax.rem(place, wide)
    gather[...] = jnp.where(
        (lane == inner * 4 + place // wide) & (inner < quarter), 1.0, 0.0).astype(BF16)

    scale = unpack(xb_recv, xb_sem)
    for m in range(2):
        for j in range(4):
            source = (at.dp if j == 0 else sources[j - 1]) + 1 - 2 * at.core
            remote(shard(m, source), shard(m, source), g_send.at[m, j], g_recv.at[m, j],
                   sibling).wait_recv()
        for k in range(4):
            first = dot(normed(m, k, scale), factors[m, 0, k]).astype(BF16)
            first = dot(first, spread[...]).astype(BF16)
            for q in range(4):
                padded[q, :, k * wide:(k + 1) * wide] = first[:, q * wide:(q + 1) * wide]
        for q in range(4):
            second = dot(gather[...], factors[m, 1, q]).astype(BF16)
            z = dot(padded[q], second)
            gates[m, q] = 1.0 / (1.0 + jnp.exp(-z))

    for m in range(2):
        pltpu.make_async_copy(r_recv.at[m], r_recv.at[m], r_sem.at[m, 1]).wait()
        parts = from_chunks(r_recv.at[m])
        outputs = []
        for k in range(4):
            mixed = dot(mix[m], parts[k].astype(BF16)).astype(BF16).astype(F32)
            y = (x_all[k] + mixed * gates[m, k]).astype(BF16).astype(F32)
            sums[m * 4 + k:m * 4 + k + 1, :] = jnp.sum(y, axis=0, keepdims=True)
            outputs.append(y)
        if m == 0:
            to_chunks(outputs, y_send)
            keep_own(y_send, y_recv, y_sem)
            send_part(y_send, y_recv, y_sem, 0, n_c // 8)

    stage = (sums, buf_y, send_y, recv_y, at.y_peer, at.y, at.n_y)
    pending += spread_out(*stage)
    send_part(y_send, y_recv, y_sem, n_c // 8, n_c // 8 * 3)
    gathered(*stage)
    own_y[...] = total_of(buf_y, at.n_y)
    stage = (own_y, buf_w, send_w, recv_w, at.w_peer, at.w, at.n_w)
    pending += spread_out(*stage)
    send_part(y_send, y_recv, y_sem, n_c // 8 * 3, n_c // 8 * 5)
    gathered(*stage)
    own_w[...] = total_of(buf_w, at.n_w) / seq_len
    stage = (own_w, buf_d, send_d, recv_d, at.d_peer, at.dp, n_d)
    pending += spread_out(*stage)
    send_part(y_send, y_recv, y_sem, n_c // 8 * 5, n_c // 8 * 7)
    gathered(*stage)
    local = []
    reps = n_d // 4
    for m in range(2):
        mine = (iota((8, 1), 0) == m * 4 + at.dp // reps).astype(F32)
        model = (iota((8, 1), 0) // 4 == m).astype(F32)
        rows, norms = [], []
        for n in range(n_d):
            pooled = buf_d[n]
            rows.append(jnp.sum(pooled * mine, axis=0, keepdims=True))
            square = jnp.sum(pooled * pooled * model, axis=0, keepdims=True)
            norms.append(jnp.sum(square, axis=1, keepdims=True))
        norm = lax.rsqrt(jnp.concatenate(norms, axis=0) / (4 * width) + 1e-06)
        head = head_refs[m][...].astype(F32)
        slot = iota((width, 1), 0) // (width // reps)
        head = jnp.where(slot == lax.rem(at.dp, reps), jnp.concatenate([head] * reps, axis=0), 0.0)
        local.append(jnp.dot(jnp.concatenate(rows, axis=0) * norm, head,
                             precision=lax.Precision.HIGHEST, preferred_element_type=F32))
    own_l[...] = jnp.concatenate(local, axis=1)
    stage = (own_l, buf_l, send_l, recv_l, at.d_peer, at.dp, n_d)
    pending += spread_out(*stage)
    send_part(y_send, y_recv, y_sem, n_c // 8 * 7, n_c - 1)
    gathered(*stage)
    logits = total_of(buf_l, n_d)
    classes = logits.shape[1] // 2
    row = iota((n_d, 1), 0)
    target = jnp.zeros((n_d, 1), jnp.int32)
    for n in range(n_d):
        target = jnp.where(row == n, target_ref[n], target)
    chosen = iota((n_d, classes), 1) == target
    losses = []
    for part in (logits[:, :classes], logits[:, classes:]):
        top = jnp.max(part, axis=1, keepdims=True)
        summed = jnp.log(jnp.sum(jnp.exp(part - top), axis=1, keepdims=True)) + top
        losses.append(summed - jnp.sum(jnp.where(chosen, part, 0.0), axis=1, keepdims=True))
    scores = losses[0] - losses[1]
    lane = iota((1, 128), 1)
    wanted = jnp.where(lane < n_d, lane, -1)
    for k in range(candidate_ref.shape[0]):
        wanted = jnp.where(lane == n_d + k, candidate_ref[k], wanted)
    score_ref[...] = jnp.sum(jnp.where(row == wanted, scores, 0.0), axis=0, keepdims=True)

    pltpu.make_async_copy(y_recv, y_recv, y_sem.at[1]).wait()
    parts = from_chunks(y_recv)
    for k in range(4):
        out_ref[:, k * width:(k + 1) * width] = parts[k].astype(BF16)

    def sent(view, sem):
        pltpu.make_async_copy(view, view, sem).wait()

    sent(xa_send.at[pl.ds(0, n_c - 1)], xa_sem.at[0])
    sent(xb_send.at[pl.ds(0, n_c - 1)], xb_sem.at[0])
    for buf, sem in ((r_send.at[0], r_sem.at[0, 0]), (r_send.at[1], r_sem.at[1, 0]),
                     (y_send, y_sem.at[0])):
        sent(buf.at[pl.ds(0, n_c // 2 - 1)], sem)
        sent(buf.at[0, 0], sem)
    for copy in pending:
        copy.wait_send()


def layer_call(ids, target, candidates, table, online, frozen, seq_len):
    n_d, n_c = lax.axis_size("dp"), lax.axis_size("ctx")
    n_x = 4 if n_c == 64 else n_c // 2
    n_w = 2 * n_x
    n_y = n_c // n_w
    feats, vocab = table.shape
    block = online[0].shape[1]
    depth, width = online[2].shape[2:]
    wide = -(-(width // 4) // 128) * 128
    n_l = -(-vocab // (2 * block)) * 2
    classes = online[4].shape[1]
    dma = pltpu.SemaphoreType.DMA
    found = (n_c, 2 * feats, block // 2)
    chunks = (n_c // 2, 2, 16, width)
    vmem, smem = pl.BlockSpec(memory_space=pltpu.VMEM), pl.BlockSpec(memory_space=pltpu.SMEM)
    return pl.pallas_call(
        functools.partial(layer_kernel, (n_d, n_c, seq_len)),
        out_shape=(jax.ShapeDtypeStruct((block, 4 * width), BF16),
                   jax.ShapeDtypeStruct((1, 128), F32)),
        in_specs=[vmem, smem, smem] + [vmem] * 11,
        out_specs=(vmem, vmem),
        scratch_shapes=[
            pltpu.VMEM((n_l * feats, block), BF16),
            pltpu.VMEM(found, BF16), pltpu.VMEM(found, BF16),
            pltpu.VMEM(found, BF16), pltpu.VMEM(found, BF16),
            pltpu.VMEM((2, n_c * feats, block // 2), F32),
            pltpu.VMEM((4, block, width), F32),
            pltpu.VMEM((2,) + chunks, BF16), pltpu.VMEM((2,) + chunks, BF16),
            pltpu.VMEM(chunks, BF16), pltpu.VMEM(chunks, BF16),
            pltpu.VMEM((2, 2, 4, depth * n_d, width), BF16),
            pltpu.VMEM((2, 4, block, width), F32),
            pltpu.VMEM((2, block, block), BF16),
            pltpu.VMEM((width, 4 * wide), BF16), pltpu.VMEM((4 * wide, width), BF16),
            pltpu.VMEM((4, block, 4 * wide), BF16),
            pltpu.VMEM((8, width), F32),
            pltpu.VMEM((n_y, 8, width), F32), pltpu.VMEM((n_w, 8, width), F32),
            pltpu.VMEM((n_d, 8, width), F32), pltpu.VMEM((n_d, n_d, 2 * classes), F32),
            pltpu.VMEM((8, width), F32), pltpu.VMEM((8, width), F32),
            pltpu.VMEM((n_d, 2 * classes), F32),
            dma((2,)), dma((2,)), dma((2, 2)), dma((2,)),
            dma((2, 3)), dma((2, 3)), dma((2, 3, max(n_x - 1, 1))), dma((2, 3, max(n_x - 1, 1))),
            dma((2, 4)), dma((2, 4)), dma((2,)),
            dma((n_y,)), dma((n_y,)), dma((n_w,)), dma((n_w,)),
            dma((n_d,)), dma((n_d,)), dma((n_d,)), dma((n_d,)),
        ],
        compiler_params=pltpu.CompilerParams(
            collective_id=1, has_side_effects=True, vmem_limit_bytes=56 * 1024 * 1024),
        name="layer",
    )(ids, target, candidates, table, *online, *frozen)


def body(
    token_ids,
    target_ids,
    candidates,
    embed_table,
    online_blocks,
    online_across,
    online_channel,
    online_gain,
    online_head,
    ref_blocks,
    ref_across,
    ref_channel,
    ref_gain,
    ref_head,
):
    n_d, n_c = lax.axis_size("dp"), lax.axis_size("ctx")
    seq_len = token_ids.shape[1]
    out, scores = layer_call(
        token_ids.reshape(n_c, seq_len // n_c),
        target_ids,
        candidates,
        embed_table,
        (online_blocks, online_across, online_channel, online_gain[None], online_head),
        (ref_blocks, ref_across, ref_channel, ref_gain[None], ref_head),
        seq_len,
    )
    return (out, scores[0, :n_d], scores[0, n_d:n_d + candidates.shape[0]])


def solution(mesh):
    in_specs = (
        P("dp", None),
        P(),
        P(),
        P("ctx", None),
        P("ctx", None, None),
        P("ctx", None, None),
        P(None, None, "dp", None),
        P(),
        P("dp", None),
        P("ctx", None, None),
        P("ctx", None, None),
        P(None, None, "dp", None),
        P(),
        P("dp", None),
    )
    out_specs = (P(("dp", "ctx"), None), P(), P())
    return jax.shard_map(body, mesh=mesh, in_specs=in_specs, out_specs=out_specs, check_vma=False)
```

time: 184 us -> 189 us (1.027)
  Pallas kernels: 167 us -> 177 us
  other arithmetic: 8.82 us -> 1.64 us
    pallas_call x1, Pallas kernels: 167 us -> 177 us  [layer_call(): pl.pallas_call(functools.partial(layer_kernel, (n_d, n_c, seq_len)), out_...]
    another operation x3 -> x0, other arithmetic: 3.04 us -> none  [the longest x1 1.55 us: body(): jnp.stack([online_across, ref_across])]
    broadcast_in_dim x0 -> x2, local copies, waits for them, and re-layouts: none -> 2.57 us  [the longest x1 1.29 us: body(): ref_gain[None]]
    squeeze x0 -> x2, local copies, waits for them, and re-layouts: none -> 2.33 us  [body(): return (out, scores[0, :n_d], scores[0, n_d:n_d + candidates.shape[0]])]
where the time goes in v2:
time: 189 us; the launch traced here: 188 us
  Pallas kernels  177 us (94%)
  local copies, waits for them, and re-layouts  8.12 us (4%)
    pallas_call x1, Pallas kernels, layer_call(): pl.pallas_call(functools.partial(layer_kernel, (n_d, n_c, seq_len)), out_...  177 us

profile of v2, /device:TPU:1, one launch (start us, length us, event | category | flops | bytes accessed | tf_op | source)
XLA Modules:
  0.0 187.7 jit_solution(10223011923752946994)
XLA Ops:
  0.6 1.3 broadcast_in_dim.6.online_gain
  1.9 1.3 broadcast_in_dim.7.frozen_gain
  3.2 0.5 broadcast.3
  3.7 1.6 reduce.3
  5.4 0.6 reshape.9.ids_ref
  6.0 177.3 %layer.1 = (bf16[256,1536]{1,0:T(8,128)(2,1)}, f32[1,128]{1,0:T(1,128)}) custom-call(s32[64,256]{1,0:T(8,128)} %reshape.9.ids_ref, s32[8]{0:T(128)} %target_ref.1, s32[4]{0:T(128)} %candidate_ref.1, bf16[24,30528]{1,0:T(8,128)(2,1)} %table_ref.1, bf16[1,256,256]{2,1,0:T(8,128)(2,1)} %online_blocks.1, bf16[4,64,64]{2,1,0:T(8,128)(2,1)} %online_across.1, ...), custom_call_target="tpu_custom_call" | custom-call | tf_op jit(solution)/shard_map/layer/pallas_call | solution.py:448
  183.3 1.2 slice_bitcast_fusion
  184.5 1.1 slice_bitcast_fusion.1
  185.7 2.1 %copy.18 = bf16[256,1536]{1,0:T(8,128)(2,1)} copy(bf16[256,1536]{1,0:T(8,128)(2,1)} %get-tuple-element.10) | data formatting | bytes 1572864

commit v3 on v2

--- a/solution.py
+++ b/solution.py
@@ -119,7 +119,7 @@
     dims, ids_ref, target_ref, candidate_ref, table_ref,
     online_blocks, online_across, online_channel, online_gain, online_head,
     frozen_blocks, frozen_across, frozen_channel, frozen_gain, frozen_head,
-    out_ref, score_ref,
+    out_ref, score_ref, picked_ref,
     tall, xa_send, xa_recv, xb_send, xb_recv, flipped, x_all, r_send, r_recv, y_send, y_recv,
     factors, gates, mix, spread, gather, padded, sums,
     buf_y, buf_w, buf_d, buf_l, own_y, own_w, own_l,
@@ -196,65 +196,54 @@
         copy.start()
         own_factors.append(copy)
 
-    def send_found(low, high, i, dest, send, recv, sems):
-        hot = jnp.where(iota((block, block), 0).astype(F32) == low, 1.0, 0.0).astype(BF16)
+    l_step = 8 if n_l % 8 == 0 else 2
+
+    def lookup(i, carry):
+        dest = at.ctx_at(n_c - 1 - i)
+        ids = ids_ref[:, pl.ds(pl.multiple_of(dest * block, block), block)]
+        low, high = lax.rem(ids, block), ids // block
+        hot = jnp.where(iota((block, block), 0) == low, 1.0, 0.0).astype(BF16)
         found = jnp.zeros((feats, block), F32)
-        picked = dot(tall[...], hot)
-        for l in range(n_l):
-            found = jnp.where(high == float(l), picked[l * feats:(l + 1) * feats], found)
-        send[dest] = jnp.concatenate([found[:, :half], found[:, half:]], axis=0).astype(BF16)
+        for start in range(0, n_l, l_step):
+            picked = dot(tall[start * feats:(start + l_step) * feats, :], hot)
+            for l in range(l_step):
+                found = jnp.where(high == start + l, picked[l * feats:(l + 1) * feats], found)
+        xa_send[dest] = jnp.concatenate([found[:, :half], found[:, half:]], axis=0).astype(BF16)
 
         @pl.when(i < n_c - 1)
         def _():
-            remote(send.at[dest], recv.at[at.ctx], sems.at[0], sems.at[1], (at.dp, dest)).start()
+            remote(xa_send.at[dest], xa_recv.at[at.ctx], xa_sem.at[0], xa_sem.at[1],
+                   (at.dp, dest)).start()
 
         @pl.when(i == n_c - 1)
         def _():
-            pltpu.make_async_copy(send.at[dest], recv.at[at.ctx], sems.at[1]).start()
-
-    def lookup_own(i, carry):
-        dest = at.ctx_at(n_c - 1 - i)
-        ids = ids_ref[pl.ds(dest, 1), :]
-        low, high = lax.rem(ids, block).astype(F32), (ids // block).astype(F32)
-        send_found(low, high, i, dest, xa_send, xa_recv, xa_sem)
+            pltpu.make_async_copy(xa_send.at[dest], xa_recv.at[at.ctx], xa_sem.at[1]).start()
+
         return carry
 
-    def lookup_across(i, carry):
-        dest = at.ctx_at(n_c - 1 - i)
-        ids = ids_ref[...]
-        both = jnp.concatenate([lax.rem(ids, block), ids // block], axis=0)
-        offset = lax.rem(iota((block, block), 1), group) + dest * group
-        pick = jnp.where(iota((block, block), 0) == offset, 1.0, 0.0).astype(BF16)
-        both = dot(both.astype(F32).astype(BF16), pick)
-        mine = iota((n_c, block), 1) // group == iota((n_c, block), 0)
-        low = jnp.sum(jnp.where(mine, both[:n_c], 0.0), axis=0, keepdims=True)
-        high = jnp.sum(jnp.where(mine, both[n_c:], 0.0), axis=0, keepdims=True)
-        send_found(low, high, i, dest, xb_send, xb_recv, xb_sem)
-        return carry
-
-    def unpack(recv, sems):
-        pltpu.make_async_copy(recv, recv, sems.at[1]).wait()
+    def unpack():
+        pltpu.make_async_copy(xa_recv, xa_recv, xa_sem.at[1]).wait()
 
         def flip(i, carry):
-            both = recv[i].astype(F32)
+            both = xa_recv[i].astype(F32)
             start = pl.multiple_of(i * feats, feats)
             flipped[0, pl.ds(start, feats), :] = both[:feats]
             flipped[1, pl.ds(start, feats), :] = both[feats:]
             return carry
 
         lax.fori_loop(0, n_c, flip, 0)
-        squares = []
         for i in range(2):
-            square = jnp.zeros((half, 1), F32)
             for k in range(4):
-                values = flipped[i, k * width:(k + 1) * width, :].T
-                square = square + jnp.sum(values * values, axis=1, keepdims=True)
-                x_all[k, i * half:(i + 1) * half, :] = values
-            squares.append(square)
-        return lax.rsqrt(jnp.concatenate(squares, axis=0) / (4 * width) + 1e-06)
+                x_all[k, i * half:(i + 1) * half, :] = flipped[i, k * width:(k + 1) * width, :].T
+
+    def norm_scale():
+        square = jnp.zeros((block, 1), F32)
+        for k in range(4):
+            square = square + jnp.sum(x_all[k] * x_all[k], axis=1, keepdims=True)
+        return lax.rsqrt(square / (4 * width) + 1e-06)
 
     def normed(m, k, scale):
-        gain = gain_refs[m][:, k * width:(k + 1) * width].astype(F32)
+        gain = gain_refs[m][k * width:(k + 1) * width].astype(F32).reshape(1, width)
         return (x_all[k] * scale * gain).astype(BF16)
 
     def send_part(send, recv, sems, first, last):
@@ -271,12 +260,12 @@
         pltpu.make_async_copy(send.at[at.ctx // 2, lax.rem(at.ctx, 2)],
                               recv.at[at.ctx // 2, lax.rem(at.ctx, 2)], sems.at[1]).start()
 
-    def within(m, scale):
-        to_chunks([dot(blocks_refs[m][0], normed(m, k, scale)) for k in range(4)], r_send.at[m])
-        send_part(r_send.at[m], r_recv.at[m], r_sem.at[m], 0, n_c - 1)
-        keep_own(r_send.at[m], r_recv.at[m], r_sem.at[m])
-
-    lax.fori_loop(0, n_c, lookup_own, 0)
+    def send_chunks(parts, send, recv, sems):
+        to_chunks(parts, send)
+        send_part(send, recv, sems, 0, n_c - 1)
+        keep_own(send, recv, sems)
+
+    lax.fori_loop(0, n_c, lookup, 0)
 
     for m in range(2):
         for j, source in enumerate(sources):
@@ -288,10 +277,12 @@
                 copy.start()
                 pending.append(copy)
 
-    scale = unpack(xa_recv, xa_sem)
-    within(0, scale)
-    lax.fori_loop(0, n_c, lookup_across, 0)
-    within(1, scale)
+    unpack()
+    send_chunks([x_all[k] for k in range(4)], xb_send, xb_recv, xb_sem)
+    scale = norm_scale()
+    for m in range(2):
+        send_chunks([dot(blocks_refs[m][0], normed(m, k, scale)) for k in range(4)],
+                    r_send.at[m], r_recv.at[m], r_sem.at[m])
 
     other = at.dp + 1 - 2 * at.core
     sibling = (other, at.ctx)
@@ -327,7 +318,11 @@
     gather[...] = jnp.where(
         (lane == inner * 4 + place // wide) & (inner < quarter), 1.0, 0.0).astype(BF16)
 
-    scale = unpack(xb_recv, xb_sem)
+    pltpu.make_async_copy(xb_recv, xb_recv, xb_sem.at[1]).wait()
+    parts = from_chunks(xb_recv)
+    for k in range(4):
+        x_all[k] = parts[k]
+    scale = norm_scale()
     for m in range(2):
         for j in range(4):
             source = (at.dp if j == 0 else sources[j - 1]) + 1 - 2 * at.core
@@ -406,11 +401,10 @@
         summed = jnp.log(jnp.sum(jnp.exp(part - top), axis=1, keepdims=True)) + top
         losses.append(summed - jnp.sum(jnp.where(chosen, part, 0.0), axis=1, keepdims=True))
     scores = losses[0] - losses[1]
-    lane = iota((1, 128), 1)
-    wanted = jnp.where(lane < n_d, lane, -1)
+    for n in range(n_d):
+        score_ref[n] = jnp.sum(jnp.where(row == n, scores, 0.0))
     for k in range(candidate_ref.shape[0]):
-        wanted = jnp.where(lane == n_d + k, candidate_ref[k], wanted)
-    score_ref[...] = jnp.sum(jnp.where(row == wanted, scores, 0.0), axis=0, keepdims=True)
+        picked_ref[k] = jnp.sum(jnp.where(row == candidate_ref[k], scores, 0.0))
 
     pltpu.make_async_copy(y_recv, y_recv, y_sem.at[1]).wait()
     parts = from_chunks(y_recv)
@@ -421,9 +415,8 @@
         pltpu.make_async_copy(view, view, sem).wait()
 
     sent(xa_send.at[pl.ds(0, n_c - 1)], xa_sem.at[0])
-    sent(xb_send.at[pl.ds(0, n_c - 1)], xb_sem.at[0])
-    for buf, sem in ((r_send.at[0], r_sem.at[0, 0]), (r_send.at[1], r_sem.at[1, 0]),
-                     (y_send, y_sem.at[0])):
+    for buf, sem in ((xb_send, xb_sem.at[0]), (r_send.at[0], r_sem.at[0, 0]),
+                     (r_send.at[1], r_sem.at[1, 0]), (y_send, y_sem.at[0])):
         sent(buf.at[pl.ds(0, n_c // 2 - 1)], sem)
         sent(buf.at[0, 0], sem)
     for copy in pending:
@@ -448,13 +441,14 @@
     return pl.pallas_call(
         functools.partial(layer_kernel, (n_d, n_c, seq_len)),
         out_shape=(jax.ShapeDtypeStruct((block, 4 * width), BF16),
-                   jax.ShapeDtypeStruct((1, 128), F32)),
+                   jax.ShapeDtypeStruct((n_d,), F32),
+                   jax.ShapeDtypeStruct(candidates.shape, F32)),
         in_specs=[vmem, smem, smem] + [vmem] * 11,
-        out_specs=(vmem, vmem),
+        out_specs=(vmem, smem, smem),
         scratch_shapes=[
             pltpu.VMEM((n_l * feats, block), BF16),
             pltpu.VMEM(found, BF16), pltpu.VMEM(found, BF16),
-            pltpu.VMEM(found, BF16), pltpu.VMEM(found, BF16),
+            pltpu.VMEM(chunks, BF16), pltpu.VMEM(chunks, BF16),
             pltpu.VMEM((2, n_c * feats, block // 2), F32),
             pltpu.VMEM((4, block, width), F32),
             pltpu.VMEM((2,) + chunks, BF16), pltpu.VMEM((2,) + chunks, BF16),
@@ -497,18 +491,15 @@
     ref_gain,
     ref_head,
 ):
-    n_d, n_c = lax.axis_size("dp"), lax.axis_size("ctx")
-    seq_len = token_ids.shape[1]
-    out, scores = layer_call(
-        token_ids.reshape(n_c, seq_len // n_c),
+    return layer_call(
+        token_ids,
         target_ids,
         candidates,
         embed_table,
-        (online_blocks, online_across, online_channel, online_gain[None], online_head),
-        (ref_blocks, ref_across, ref_channel, ref_gain[None], ref_head),
-        seq_len,
+        (online_blocks, online_across, online_channel, online_gain, online_head),
+        (ref_blocks, ref_across, ref_channel, ref_gain, ref_head),
+        token_ids.shape[1],
     )
-    return (out, scores[0, :n_d], scores[0, n_d:n_d + candidates.shape[0]])
 
 
 def solution(mesh):

time: 189 us -> 155 us (0.82)
  Pallas kernels: 177 us -> 151 us
  local copies, waits for them, and re-layouts: 8.12 us -> 3.1 us
    pallas_call x1, Pallas kernels: 177 us -> 151 us  [layer_call(): pl.pallas_call(functools.partial(layer_kernel, (n_d, n_c, seq_len)), out_...]
    broadcast_in_dim x2 -> x0, local copies, waits for them, and re-layouts: 2.57 us -> none  [the longest x1 1.29 us: body(): ref_gain[None]]
    squeeze x2 -> x0, local copies, waits for them, and re-layouts: 2.33 us -> none  [body(): return (out, scores[0, :n_d], scores[0, n_d:n_d + candidates.shape[0]])]
where the time goes in v3:
time: 155 us
  Pallas kernels  151 us (97%)
  local copies, waits for them, and re-layouts  3.1 us (2%)
    pallas_call x1, Pallas kernels, layer_call(): pl.pallas_call(functools.partial(layer_kernel, (n_d, n_c, seq_len)), out_...  151 us

profile of v3, /device:TPU:1, one launch (start us, length us, event | category | flops | bytes accessed | tf_op | source)
XLA Modules:
  0.0 155.0 jit_solution(14272191470686170120)
XLA Ops:
  0.6 151.2 %layer.1 = (bf16[256,1536]{1,0:T(8,128)(2,1)}, f32[8]{0:T(128)}, f32[4]{0:T(128)}) custom-call(s32[1,16384]{1,0:T(1,128)} %ids_ref.1, s32[8]{0:T(128)} %target_ref.1, s32[4]{0:T(128)} %candidate_ref.1, bf16[24,30528]{1,0:T(8,128)(2,1)} %table_ref.1, bf16[1,256,256]{2,1,0:T(8,128)(2,1)} %online_blocks.1, bf16[4,64,64]{2,1,0:T(8,128)(2,1)} %online_across.1, ...), custom_call_target="tpu_custom_call" | custom-call | tf_op jit(solution)/shard_map/layer/pallas_call | solution.py:441
  151.9 0.0 copy-start.1
  151.9 0.0 copy-start
  151.9 2.1 %copy.20 = bf16[256,1536]{1,0:T(8,128)(2,1)} copy(bf16[256,1536]{1,0:T(8,128)(2,1)} %get-tuple-element.6) | data formatting | bytes 1572864
  153.9 0.0 copy-done.1
  153.9 0.5 copy.21
  154.5 0.0 copy-done
  154.5 0.5 copy.22
Async XLA Ops:
  151.9 2.1 %copy-start.1 = (f32[8]{0:T(128)S(1)}, f32[8]{0:T(128)}, u32[]{:S(2)}) copy-start(f32[8]{0:T(128)} %get-tuple-element.7) | copy-start | bytes 100
  151.9 2.6 %copy-start = (f32[4]{0:T(128)S(1)}, f32[4]{0:T(128)}, u32[]{:S(2)}) copy-start(f32[4]{0:T(128)} %get-tuple-element.8) | copy-start | bytes 52

commit v4 on v3

--- a/solution.py
+++ b/solution.py
@@ -197,27 +197,36 @@
         own_factors.append(copy)
 
     l_step = 8 if n_l % 8 == 0 else 2
+    per_step = 2
 
     def lookup(i, carry):
-        dest = at.ctx_at(n_c - 1 - i)
-        ids = ids_ref[:, pl.ds(pl.multiple_of(dest * block, block), block)]
+        dests = [at.ctx_at(n_c - 1 - (i * per_step + j)) for j in range(per_step)]
+        ids = jnp.concatenate(
+            [ids_ref[:, pl.ds(pl.multiple_of(d * block, block), block)] for d in dests], axis=1)
         low, high = lax.rem(ids, block), ids // block
-        hot = jnp.where(iota((block, block), 0) == low, 1.0, 0.0).astype(BF16)
-        found = jnp.zeros((feats, block), F32)
+        hot = jnp.where(iota((block, per_step * block), 0) == low, 1.0, 0.0).astype(BF16)
+        found = jnp.zeros((feats, per_step * block), F32)
         for start in range(0, n_l, l_step):
             picked = dot(tall[start * feats:(start + l_step) * feats, :], hot)
             for l in range(l_step):
                 found = jnp.where(high == start + l, picked[l * feats:(l + 1) * feats], found)
-        xa_send[dest] = jnp.concatenate([found[:, :half], found[:, half:]], axis=0).astype(BF16)
-
-        @pl.when(i < n_c - 1)
-        def _():
-            remote(xa_send.at[dest], xa_recv.at[at.ctx], xa_sem.at[0], xa_sem.at[1],
-                   (at.dp, dest)).start()
-
-        @pl.when(i == n_c - 1)
-        def _():
-            pltpu.make_async_copy(xa_send.at[dest], xa_recv.at[at.ctx], xa_sem.at[1]).start()
+        for j, dest in enumerate(dests):
+            mine = found[:, j * block:(j + 1) * block]
+            xa_send[dest] = jnp.concatenate([mine[:, :half], mine[:, half:]], axis=0).astype(BF16)
+
+            def send(dest=dest):
+                remote(xa_send.at[dest], xa_recv.at[at.ctx], xa_sem.at[0], xa_sem.at[1],
+                       (at.dp, dest)).start()
+
+            if j < per_step - 1:
+                send()
+            else:
+                pl.when(i < n_c // per_step - 1)(send)
+
+                @pl.when(i == n_c // per_step - 1)
+                def _():
+                    pltpu.make_async_copy(
+                        xa_send.at[dest], xa_recv.at[at.ctx], xa_sem.at[1]).start()
 
         return carry
 
@@ -265,7 +274,9 @@
         send_part(send, recv, sems, 0, n_c - 1)
         keep_own(send, recv, sems)
 
-    lax.fori_loop(0, n_c, lookup, 0)
+    n_steps = n_c // per_step
+    first_stop, second_stop = n_steps // 4, n_steps * 7 // 8
+    lax.fori_loop(0, first_stop, lookup, 0)
 
     for m in range(2):
         for j, source in enumerate(sources):
@@ -277,12 +288,7 @@
                 copy.start()
                 pending.append(copy)
 
-    unpack()
-    send_chunks([x_all[k] for k in range(4)], xb_send, xb_recv, xb_sem)
-    scale = norm_scale()
-    for m in range(2):
-        send_chunks([dot(blocks_refs[m][0], normed(m, k, scale)) for k in range(4)],
-                    r_send.at[m], r_recv.at[m], r_sem.at[m])
+    lax.fori_loop(first_stop, second_stop, lookup, 0)
 
     other = at.dp + 1 - 2 * at.core
     sibling = (other, at.ctx)
@@ -298,6 +304,15 @@
                           sibling)
             copy.start()
             pending.append(copy)
+
+    lax.fori_loop(second_stop, n_steps, lookup, 0)
+
+    unpack()
+    send_chunks([x_all[k] for k in range(4)], xb_send, xb_recv, xb_sem)
+    scale = norm_scale()
+    for m in range(2):
+        send_chunks([dot(blocks_refs[m][0], normed(m, k, scale)) for k in range(4)],
+                    r_send.at[m], r_recv.at[m], r_sem.at[m])
 
     tall_one = jnp.where(iota((block, n_c), 0) // group == iota((block, n_c), 1), 1.0, 0.0)
     wide_one = jnp.where(iota((n_c, block), 1) // group == iota((n_c, block), 0), 1.0, 0.0)
@@ -350,21 +365,21 @@
         if m == 0:
             to_chunks(outputs, y_send)
             keep_own(y_send, y_recv, y_sem)
-            send_part(y_send, y_recv, y_sem, 0, n_c // 8)
+            send_part(y_send, y_recv, y_sem, 0, n_c // 8 * 3)
 
     stage = (sums, buf_y, send_y, recv_y, at.y_peer, at.y, at.n_y)
     pending += spread_out(*stage)
-    send_part(y_send, y_recv, y_sem, n_c // 8, n_c // 8 * 3)
+    send_part(y_send, y_recv, y_sem, n_c // 8 * 3, n_c // 8 * 5)
     gathered(*stage)
     own_y[...] = total_of(buf_y, at.n_y)
     stage = (own_y, buf_w, send_w, recv_w, at.w_peer, at.w, at.n_w)
     pending += spread_out(*stage)
-    send_part(y_send, y_recv, y_sem, n_c // 8 * 3, n_c // 8 * 5)
+    send_part(y_send, y_recv, y_sem, n_c // 8 * 5, n_c // 8 * 6)
     gathered(*stage)
     own_w[...] = total_of(buf_w, at.n_w) / seq_len
     stage = (own_w, buf_d, send_d, recv_d, at.d_peer, at.dp, n_d)
     pending += spread_out(*stage)
-    send_part(y_send, y_recv, y_sem, n_c // 8 * 5, n_c // 8 * 7)
+    send_part(y_send, y_recv, y_sem, n_c // 8 * 6, n_c // 8 * 7)
     gathered(*stage)
     local = []
     reps = n_d // 4

time: 155 us -> 157 us (1.013)
  Pallas kernels: 151 us -> 153 us
where the time goes in v4:
time: 157 us; the launch traced here: 156 us
  Pallas kernels  153 us (97%)
  local copies, waits for them, and re-layouts  3.1 us (2%)
    pallas_call x1, Pallas kernels, layer_call(): pl.pallas_call(functools.partial(layer_kernel, (n_d, n_c, seq_len)), out_...  153 us

profile of v4, /device:TPU:1, one launch (start us, length us, event | category | flops | bytes accessed | tf_op | source)
XLA Modules:
  0.0 156.4 jit_solution(9190665606150321081)
XLA Ops:
  0.6 152.7 %layer.1 = (bf16[256,1536]{1,0:T(8,128)(2,1)}, f32[8]{0:T(128)}, f32[4]{0:T(128)}) custom-call(s32[1,16384]{1,0:T(1,128)} %ids_ref.1, s32[8]{0:T(128)} %target_ref.1, s32[4]{0:T(128)} %candidate_ref.1, bf16[24,30528]{1,0:T(8,128)(2,1)} %table_ref.1, bf16[1,256,256]{2,1,0:T(8,128)(2,1)} %online_blocks.1, bf16[4,64,64]{2,1,0:T(8,128)(2,1)} %online_across.1, ...), custom_call_target="tpu_custom_call" | custom-call | tf_op jit(solution)/shard_map/layer/pallas_call | solution.py:456
  153.3 0.0 copy-start.1
  153.3 0.0 copy-start
  153.3 2.1 %copy.20 = bf16[256,1536]{1,0:T(8,128)(2,1)} copy(bf16[256,1536]{1,0:T(8,128)(2,1)} %get-tuple-element.6) | data formatting | bytes 1572864
  155.4 0.0 copy-done.1
  155.4 0.5 copy.21
  155.9 0.0 copy-done
  155.9 0.5 copy.22
Async XLA Ops:
  153.3 2.1 %copy-start.1 = (f32[8]{0:T(128)S(1)}, f32[8]{0:T(128)}, u32[]{:S(2)}) copy-start(f32[8]{0:T(128)} %get-tuple-element.7) | copy-start | bytes 100
  153.3 2.6 %copy-start = (f32[4]{0:T(128)S(1)}, f32[4]{0:T(128)}, u32[]{:S(2)}) copy-start(f32[4]{0:T(128)} %get-tuple-element.8) | copy-start | bytes 52

commit v5 on v4

--- a/solution.py
+++ b/solution.py
@@ -171,8 +171,6 @@
         tall[full * 2 * feats:, :] = jnp.concatenate(
             [left[:, :block], left[:, block:]], axis=0).astype(BF16)
 
-    pl.semaphore_wait(barrier, n_c - 1 + n_d - 1 + 4)
-
     n_k = 4 // at.n_x
 
     def shard(m, dp, x=None):
@@ -184,12 +182,6 @@
     steps = (1, n_z - 1, lax.rem(2 + at.core * (n_z - 4), n_z))
     sources = [at.z_at(n_z - step)[0] for step in steps]
     pending = []
-    for m in range(2):
-        for j, step in enumerate(steps):
-            copy = remote(channel_refs[m].at[:, pl.ds(at.x * n_k, n_k)], shard(m, at.dp, at.x),
-                          f_send.at[m, j], f_recv.at[m, j], at.z_at(step))
-            copy.start()
-            pending.append(copy)
     own_factors = []
     for m in range(2):
         copy = pltpu.make_async_copy(channel_refs[m], shard(m, at.dp), local_sem.at[m])
@@ -199,7 +191,23 @@
     l_step = 8 if n_l % 8 == 0 else 2
     per_step = 2
 
-    def lookup(i, carry):
+    def send_found(i):
+        dest = at.ctx_at(n_c - 1 - i)
+
+        @pl.when(i < n_c - 1)
+        def _():
+            remote(xa_send.at[dest], xa_recv.at[at.ctx], xa_sem.at[0], xa_sem.at[1],
+                   (at.dp, dest)).start()
+
+        @pl.when(i == n_c - 1)
+        def _():
+            pltpu.make_async_copy(xa_send.at[dest], xa_recv.at[at.ctx], xa_sem.at[1]).start()
+
+    def send_early(i, carry):
+        send_found(i)
+        return carry
+
+    def lookup(i, carry, sending=True):
         dests = [at.ctx_at(n_c - 1 - (i * per_step + j)) for j in range(per_step)]
         ids = jnp.concatenate(
             [ids_ref[:, pl.ds(pl.multiple_of(d * block, block), block)] for d in dests], axis=1)
@@ -214,19 +222,8 @@
             mine = found[:, j * block:(j + 1) * block]
             xa_send[dest] = jnp.concatenate([mine[:, :half], mine[:, half:]], axis=0).astype(BF16)
 
-            def send(dest=dest):
-                remote(xa_send.at[dest], xa_recv.at[at.ctx], xa_sem.at[0], xa_sem.at[1],
-                       (at.dp, dest)).start()
-
-            if j < per_step - 1:
-                send()
-            else:
-                pl.when(i < n_c // per_step - 1)(send)
-
-                @pl.when(i == n_c // per_step - 1)
-                def _():
-                    pltpu.make_async_copy(
-                        xa_send.at[dest], xa_recv.at[at.ctx], xa_sem.at[1]).start()
+            if sending:
+                send_found(i * per_step + j)
 
         return carry
 
@@ -275,9 +272,22 @@
         keep_own(send, recv, sems)
 
     n_steps = n_c // per_step
-    first_stop, second_stop = n_steps // 4, n_steps * 7 // 8
-    lax.fori_loop(0, first_stop, lookup, 0)
-
+    early = n_steps // 2
+
+    lax.fori_loop(0, early, functools.partial(lookup, sending=False), 0)
+    pl.semaphore_wait(barrier, n_c - 1 + n_d - 1 + 4)
+    lax.fori_loop(0, early * per_step, send_early, 0)
+    lax.fori_loop(early, n_steps, lookup, 0)
+
+    for m in range(2):
+        for j, step in enumerate(steps):
+            copy = remote(channel_refs[m].at[:, pl.ds(at.x * n_k, n_k)], shard(m, at.dp, at.x),
+                          f_send.at[m, j], f_recv.at[m, j], at.z_at(step))
+            copy.start()
+            pending.append(copy)
+
+    unpack()
+    send_chunks([x_all[k] for k in range(4)], xb_send, xb_recv, xb_sem)
     for m in range(2):
         for j, source in enumerate(sources):
             remote(shard(m, source, at.x), shard(m, source, at.x), f_send.at[m, j],
@@ -288,7 +298,12 @@
                 copy.start()
                 pending.append(copy)
 
-    lax.fori_loop(first_stop, second_stop, lookup, 0)
+    scale = norm_scale()
+    def within(m):
+        send_chunks([dot(blocks_refs[m][0], normed(m, k, scale)) for k in range(4)],
+                    r_send.at[m], r_recv.at[m], r_sem.at[m])
+
+    within(0)
 
     other = at.dp + 1 - 2 * at.core
     sibling = (other, at.ctx)
@@ -305,14 +320,8 @@
             copy.start()
             pending.append(copy)
 
-    lax.fori_loop(second_stop, n_steps, lookup, 0)
-
-    unpack()
-    send_chunks([x_all[k] for k in range(4)], xb_send, xb_recv, xb_sem)
-    scale = norm_scale()
-    for m in range(2):
-        send_chunks([dot(blocks_refs[m][0], normed(m, k, scale)) for k in range(4)],
-                    r_send.at[m], r_recv.at[m], r_sem.at[m])
+    within(1)
+
 
     tall_one = jnp.where(iota((block, n_c), 0) // group == iota((block, n_c), 1), 1.0, 0.0)
     wide_one = jnp.where(iota((n_c, block), 1) // group == iota((n_c, block), 0), 1.0, 0.0)

time: 157 us -> 155 us (0.987)
  Pallas kernels: 153 us -> 151 us
where the time goes in v5:
time: 155 us
  Pallas kernels  151 us (97%)
  local copies, waits for them, and re-layouts  3.1 us (2%)
    pallas_call x1, Pallas kernels, layer_call(): pl.pallas_call(functools.partial(layer_kernel, (n_d, n_c, seq_len)), out_...  151 us

profile of v5, /device:TPU:1, one launch (start us, length us, event | category | flops | bytes accessed | tf_op | source)
XLA Modules:
  0.0 155.2 jit_solution(15732297893650475969)
XLA Ops:
  0.6 151.4 %layer.1 = (bf16[256,1536]{1,0:T(8,128)(2,1)}, f32[8]{0:T(128)}, f32[4]{0:T(128)}) custom-call(s32[1,16384]{1,0:T(1,128)} %ids_ref.1, s32[8]{0:T(128)} %target_ref.1, s32[4]{0:T(128)} %candidate_ref.1, bf16[24,30528]{1,0:T(8,128)(2,1)} %table_ref.1, bf16[1,256,256]{2,1,0:T(8,128)(2,1)} %online_blocks.1, bf16[4,64,64]{2,1,0:T(8,128)(2,1)} %online_across.1, ...), custom_call_target="tpu_custom_call" | custom-call | tf_op jit(solution)/shard_map/layer/pallas_call | solution.py:465
  152.1 0.0 copy-start.1
  152.1 0.0 copy-start
  152.1 2.1 %copy.20 = bf16[256,1536]{1,0:T(8,128)(2,1)} copy(bf16[256,1536]{1,0:T(8,128)(2,1)} %get-tuple-element.6) | data formatting | bytes 1572864
  154.2 0.0 copy-done.1
  154.2 0.5 copy.21
  154.7 0.0 copy-done
  154.7 0.5 copy.22
Async XLA Ops:
  152.1 2.1 %copy-start.1 = (f32[8]{0:T(128)S(1)}, f32[8]{0:T(128)}, u32[]{:S(2)}) copy-start(f32[8]{0:T(128)} %get-tuple-element.7) | copy-start | bytes 100
  152.1 2.6 %copy-start = (f32[4]{0:T(128)S(1)}, f32[4]{0:T(128)}, u32[]{:S(2)}) copy-start(f32[4]{0:T(128)} %get-tuple-element.8) | copy-start | bytes 52

commit v6 on v5

--- a/solution.py
+++ b/solution.py
@@ -35,9 +35,9 @@
         self.z = self.z_hi * self.z_lo_size + self.z_lo
 
     def ctx_at(self, o):
-        step_y = lax.rem(lax.rem(o, self.n_y) * 3, self.n_y)
-        rest = o // self.n_y
-        step_z, step_x = lax.rem(rest, 2), rest // 2
+        step_z, rest = lax.rem(o, 2), o // 2
+        step_y = lax.rem(rest * 3, self.n_y)
+        step_x = lax.rem(rest // self.n_y + lax.rem(rest, self.n_y), self.n_x)
         y = lax.rem(self.y + step_y, self.n_y)
         z_hi = lax.rem(self.z_hi + step_z, 2)
         x = lax.rem(self.x + step_x, self.n_x)

time: 155 us -> 158 us (1.019)
  Pallas kernels: 151 us -> 153 us
    pallas_call x1, Pallas kernels: 151 us -> 153 us  [layer_call(): pl.pallas_call(functools.partial(layer_kernel, (n_d, n_c, seq_len)), out_...]
where the time goes in v6:
time: 158 us; the launch traced here: 157 us
  Pallas kernels  153 us (97%)
  local copies, waits for them, and re-layouts  3.1 us (2%)
    pallas_call x1, Pallas kernels, layer_call(): pl.pallas_call(functools.partial(layer_kernel, (n_d, n_c, seq_len)), out_...  153 us

profile of v6, /device:TPU:1, one launch (start us, length us, event | category | flops | bytes accessed | tf_op | source)
XLA Modules:
  0.0 157.2 jit_solution(18269176366637517121)
XLA Ops:
  0.6 153.4 %layer.1 = (bf16[256,1536]{1,0:T(8,128)(2,1)}, f32[8]{0:T(128)}, f32[4]{0:T(128)}) custom-call(s32[1,16384]{1,0:T(1,128)} %ids_ref.1, s32[8]{0:T(128)} %target_ref.1, s32[4]{0:T(128)} %candidate_ref.1, bf16[24,30528]{1,0:T(8,128)(2,1)} %table_ref.1, bf16[1,256,256]{2,1,0:T(8,128)(2,1)} %online_blocks.1, bf16[4,64,64]{2,1,0:T(8,128)(2,1)} %online_across.1, ...), custom_call_target="tpu_custom_call" | custom-call | tf_op jit(solution)/shard_map/layer/pallas_call | solution.py:465
  154.1 0.0 copy-start.1
  154.1 0.0 copy-start
  154.1 2.1 %copy.20 = bf16[256,1536]{1,0:T(8,128)(2,1)} copy(bf16[256,1536]{1,0:T(8,128)(2,1)} %get-tuple-element.6) | data formatting | bytes 1572864
  156.2 0.0 copy-done.1
  156.2 0.5 copy.21
  156.7 0.0 copy-done
  156.7 0.5 copy.22
Async XLA Ops:
  154.1 2.1 %copy-start.1 = (f32[8]{0:T(128)S(1)}, f32[8]{0:T(128)}, u32[]{:S(2)}) copy-start(f32[8]{0:T(128)} %get-tuple-element.7) | copy-start | bytes 100
  154.1 2.6 %copy-start = (f32[4]{0:T(128)S(1)}, f32[4]{0:T(128)}, u32[]{:S(2)}) copy-start(f32[4]{0:T(128)} %get-tuple-element.8) | copy-start | bytes 52
